TPU v7x, 32 devices: a whole 2x2x4 slice. The times are simulated.
32 devices in a mesh: src: 2 (over x), space: 16 (over z, y, core).
Axes of the slice: x: 2, y: 2, z: 4, core: 2. Of those that a mesh axis runs over, the one named last changes fastest.
Arguments:
- fwd_current: float32 [2, 3, 128, 64, 128], P('src', None, 'space'), may hold values from -6 to 6
- adj_current: float32 [2, 3, 128, 64, 128], P('src', None, 'space'), may hold values from -6 to 6
- inv_eps: float32 [128, 64, 128], P('space'), may hold values from 0.25 to 1
- wavelength: int32 [2], P('src'), may hold values from 0 to 15
- footprint: int32 [128, 64], P('space', 'src'), may hold values from 0 to 511, as said below
Outputs:
- design_grad: float32 [512, 128], P(('src', 'space'))
Inputs may be any that keep to these rules, and one draw needn't show every extreme that they name: `footprint`: A column (x, y) whose y lies in the i-th block of 32 cells names a pixel of the pixel blocks i * 16 to (i + 1) * 16 - 1, a pixel block being 16 consecutive pixels. Among the 256 columns of one slab of 8 cells in x and one block in y, at most 32 name pixels of any one pixel block; in each group i one pixel block receives exactly 32 columns from every slab.
All inputs are finite; a program needn't handle non-finite values.
Results may differ from a plain program's by a relative error of at most 0.0003.
Values sent between devices are 32-bit elements; how exact they have to be, the bound alone decides.
A program may use at most 64 MiB of HBM per device.

v0:
```python
import jax
import jax.numpy as jnp
from jax import lax
from jax.sharding import PartitionSpec as P

ITERS = 4
PIX_DEV = 16


COURANT = 0.5


def passed_along(block, axis, distance):
    devices = range(lax.axis_size(axis))
    route = [(i - distance, i) for i in devices if i - distance in devices]
    return lax.ppermute(block, axis, route)


def roll_fwd(field, axis):
    return jnp.roll(field, -1, axis) - field


def roll_back(field, axis):
    return field - jnp.roll(field, 1, axis)


def curl_electric(parts, ahead):
    grad_y = jnp.concatenate([parts[1][:, 1:], ahead[0]], axis=1) - parts[1]
    grad_z = jnp.concatenate([parts[2][:, 1:], ahead[1]], axis=1) - parts[2]
    return (
        roll_fwd(parts[2], 2) - roll_fwd(parts[1], 3),
        roll_fwd(parts[0], 3) - grad_z,
        grad_y - roll_fwd(parts[0], 2),
    )


def curl_magnetic(parts, behind):
    grad_y = parts[1] - jnp.concatenate([behind[0], parts[1][:, :-1]], axis=1)
    grad_z = parts[2] - jnp.concatenate([behind[1], parts[2][:, :-1]], axis=1)
    return (
        roll_back(parts[2], 2) - roll_back(parts[1], 3),
        roll_back(parts[0], 3) - grad_z,
        grad_y - roll_back(parts[0], 2),
    )


def run_fields(current, signals, inv_eps):
    zero = jnp.zeros((current.shape[0],) + current.shape[2:], jnp.float32)
    electric = (zero, zero, zero)
    magnetic = (zero, zero, zero)
    stored = []
    for step in range(ITERS):
        front = jnp.stack([electric[1][:, 0:1], electric[2][:, 0:1]])
        ahead = passed_along(front, "space", -1)
        curl_e = curl_electric(electric, ahead)
        magnetic = tuple((magnetic[k] - COURANT * curl_e[k] for k in range(3)))
        rear = jnp.stack([magnetic[1][:, -1:], magnetic[2][:, -1:]])
        behind = passed_along(rear, "space", 1)
        curl_h = curl_magnetic(magnetic, behind)
        signal = signals[step][:, None, None, None]
        electric = tuple(
            (
                electric[k] + COURANT * inv_eps[None] * (curl_h[k] - current[:, k] * signal)
                for k in range(3)
            )
        )
        stored.append(electric)
    return stored


def per_device(fwd_current, adj_current, inv_eps, wavelength, footprint):
    omegas = 0.25 + 0.05 * wavelength.astype(jnp.float32)
    sin_signals = [jnp.sin(omegas * (step + 1.0)) for step in range(ITERS)]
    cos_signals = [jnp.cos(omegas * (step + 1.0)) for step in range(ITERS)]
    forward = run_fields(fwd_current, sin_signals, inv_eps)
    adjoint = run_fields(adj_current, cos_signals, inv_eps)
    local_grad = jnp.zeros(inv_eps.shape, jnp.float32)
    for step in range(ITERS):
        for k in range(3):
            local_grad = local_grad + jnp.sum(
                forward[step][k] * adjoint[ITERS - 1 - step][k], axis=0
            )
    summed = lax.psum(local_grad, "src")
    width = footprint.shape[1]
    share = lax.dynamic_slice_in_dim(summed, lax.axis_index("src") * width, width, 1)
    depth = share.shape[2]
    row_count = footprint.shape[0] * footprint.shape[1]
    columns = share.reshape(row_count, depth)
    pixel_ids = footprint.reshape(row_count)
    owners = lax.axis_size("space")
    capacity = max(2, (2 * row_count + owners - 1) // owners)
    target = pixel_ids // PIX_DEV % owners
    onehot = (target[:, None] == jnp.arange(owners, dtype=jnp.int32)[None, :]).astype(jnp.int32)
    ranks = jnp.sum(onehot * (jnp.cumsum(onehot, axis=0) - 1), axis=1)
    slot_of = target * capacity + ranks
    slot_count = owners * capacity
    select = slot_of[None, :] == jnp.arange(slot_count, dtype=jnp.int32)[:, None]
    packed = jnp.dot(
        select.astype(jnp.float32),
        columns,
        preferred_element_type=jnp.float32,
        precision=lax.Precision.HIGHEST,
    )
    packed_ids = jnp.max(jnp.where(select, (pixel_ids % PIX_DEV)[None, :], -1), axis=1)
    arrived, arrived_ids = (
        lax.all_to_all(
            packed.reshape(owners, capacity, depth),
            "space",
            split_axis=0,
            concat_axis=0,
            tiled=True,
        ),
        lax.all_to_all(
            packed_ids.reshape(owners, capacity), "space", split_axis=0, concat_axis=0, tiled=True
        ),
    )
    flat_vals = arrived.reshape(slot_count, depth)
    flat_ids = arrived_ids.reshape(slot_count)
    gather_rows = (flat_ids[None, :] == jnp.arange(PIX_DEV, dtype=jnp.int32)[:, None]).astype(
        jnp.float32
    )
    return jnp.dot(
        gather_rows, flat_vals, preferred_element_type=jnp.float32, precision=lax.Precision.HIGHEST
    )


def solution(mesh):
    in_specs = (
        P("src", None, "space", None, None),
        P("src", None, "space", None, None),
        P("space", None, None),
        P("src"),
        P("space", "src"),
    )
    out_specs = P(("src", "space"), None)
    return jax.shard_map(
        per_device, mesh=mesh, in_specs=in_specs, out_specs=out_specs, check_vma=False
    )
```

profile of v0, /device:TPU:0, one launch (start us, length us, event | category | flops | bytes accessed | tf_op | source)
XLA Modules:
  0.0 128.3 jit_solution(2380955290129045408)
XLA Ops:
  6.5 1.3 collective-permute-start
  9.1 0.4 copy-done.5
  9.8 0.6 reduce-window.6
  10.4 0.2 slice_reduce_fusion
  10.6 0.6 copy-done.6
  11.4 4.2 %collective-permute-start.1 = (f32[2,1,1,64,128]{4,3,2,1,0:T(8,128)S(1)}, f32[2,1,1,64,128]{4,3,2,1,0:T(8,128)S(1)}, u32[]{:S(2)}, u32[]{:S(2)}) collective-permute-start(f32[2,1,1,64,128]{4,3,2,1,0:T(8,128)S(1)} %pad_maximum_fusion), channel_id=1, source_target_pairs={{0,1},{1,2},{2,3},{3,4},{4,5},{5,6},{6,7},{7,8},{8,9},{9,10},{10,1... | collective-permute-start | bytes 196616 | tf_op jit(solution)/shard_map/ppermute | solution.py:16
  15.9 0.1 slice.839
  16.0 0.4 collective-permute-done.1
  16.4 0.5 copy-done.2
  17.0 0.3 fusion.151
  17.5 0.1 slice.865
  17.7 0.1 fusion.150
  17.9 0.6 copy-done.3
  18.5 0.5 copy-done.1
  19.1 0.3 fusion.149
  19.8 1.4 %collective-permute-start.2 = (f32[2,1,1,64,128]{4,3,2,1,0:T(8,128)S(1)}, f32[2,1,1,64,128]{4,3,2,1,0:T(8,128)S(1)}, u32[]{:S(2)}, u32[]{:S(2)}) collective-permute-start(f32[2,1,1,64,128]{4,3,2,1,0:T(8,128)S(1)} %pad_maximum_fusion.1), channel_id=1, source_target_pairs={{1,0},{2,1},{3,2},{4,3},{5,4},{6,5},{7,6},{8,7},{9,8},{10,9},{11,1... | collective-permute-start | bytes 196616 | tf_op jit(solution)/shard_map/ppermute | solution.py:16
  21.3 1.3 %collective-permute-start.8 = (f32[2,1,1,64,128]{4,3,2,1,0:T(8,128)S(1)}, f32[2,1,1,64,128]{4,3,2,1,0:T(8,128)S(1)}, u32[]{:S(2)}, u32[]{:S(2)}) collective-permute-start(f32[2,1,1,64,128]{4,3,2,1,0:T(8,128)S(1)} %pad_maximum_fusion.7), channel_id=1, source_target_pairs={{1,0},{2,1},{3,2},{4,3},{5,4},{6,5},{7,6},{8,7},{9,8},{10,9},{11,1... | collective-permute-start | bytes 196616 | tf_op jit(solution)/shard_map/ppermute | solution.py:16
  22.6 1.5 %collective-permute-done.2 = f32[2,1,1,64,128]{4,3,2,1,0:T(8,128)S(1)} collective-permute-done((f32[2,1,1,64,128]{4,3,2,1,0:T(8,128)S(1)}, f32[2,1,1,64,128]{4,3,2,1,0:T(8,128)S(1)}, u32[]{:S(2)}, u32[]{:S(2)}) %collective-permute-start.2) | collective-permute-done | bytes 65568 | tf_op jit(solution)/shard_map/ppermute | solution.py:16
  24.1 0.4 fusion.17
  24.5 0.1 slice.861
  24.8 1.1 collective-permute-done.8
  26.0 0.4 fusion.94
  26.8 5.4 %collective-permute-start.3 = (f32[2,1,1,64,128]{4,3,2,1,0:T(8,128)S(1)}, f32[2,1,1,64,128]{4,3,2,1,0:T(8,128)S(1)}, u32[]{:S(2)}, u32[]{:S(2)}) collective-permute-start(f32[2,1,1,64,128]{4,3,2,1,0:T(8,128)S(1)} %pad_maximum_fusion.2), channel_id=1, source_target_pairs={{0,1},{1,2},{2,3},{3,4},{4,5},{5,6},{6,7},{7,8},{8,9},{9,10},{10,1... | collective-permute-start | bytes 196616 | tf_op jit(solution)/shard_map/ppermute | solution.py:16
  32.2 1.9 %collective-permute-start.9 = (f32[2,1,1,64,128]{4,3,2,1,0:T(8,128)S(1)}, f32[2,1,1,64,128]{4,3,2,1,0:T(8,128)S(1)}, u32[]{:S(2)}, u32[]{:S(2)}) collective-permute-start(f32[2,1,1,64,128]{4,3,2,1,0:T(8,128)S(1)} %pad_maximum_fusion.8), channel_id=1, source_target_pairs={{0,1},{1,2},{2,3},{3,4},{4,5},{5,6},{6,7},{7,8},{8,9},{9,10},{10,1... | collective-permute-start | bytes 196616 | tf_op jit(solution)/shard_map/ppermute | solution.py:16
  34.1 0.4 fusion.11
  34.5 0.2 fusion.21
  34.8 1.3 %collective-permute-start.4 = (f32[2,1,1,64,128]{4,3,2,1,0:T(8,128)S(1)}, f32[2,1,1,64,128]{4,3,2,1,0:T(8,128)S(1)}, u32[]{:S(2)}, u32[]{:S(2)}) collective-permute-start(f32[2,1,1,64,128]{4,3,2,1,0:T(8,128)S(1)} %pad_maximum_fusion.3), channel_id=1, source_target_pairs={{1,0},{2,1},{3,2},{4,3},{5,4},{6,5},{7,6},{8,7},{9,8},{10,9},{11,1... | collective-permute-start | bytes 196616 | tf_op jit(solution)/shard_map/ppermute | solution.py:16
  36.1 0.4 fusion.98
  37.0 3.8 %collective-permute-done.4 = f32[2,1,1,64,128]{4,3,2,1,0:T(8,128)S(1)} collective-permute-done((f32[2,1,1,64,128]{4,3,2,1,0:T(8,128)S(1)}, f32[2,1,1,64,128]{4,3,2,1,0:T(8,128)S(1)}, u32[]{:S(2)}, u32[]{:S(2)}) %collective-permute-start.4) | collective-permute-done | bytes 65568 | tf_op jit(solution)/shard_map/ppermute | solution.py:16
  40.8 0.4 fusion.38
  41.3 4.8 %collective-permute-start.5 = (f32[2,1,1,64,128]{4,3,2,1,0:T(8,128)S(1)}, f32[2,1,1,64,128]{4,3,2,1,0:T(8,128)S(1)}, u32[]{:S(2)}, u32[]{:S(2)}) collective-permute-start(f32[2,1,1,64,128]{4,3,2,1,0:T(8,128)S(1)} %pad_maximum_fusion.4), channel_id=1, source_target_pairs={{0,1},{1,2},{2,3},{3,4},{4,5},{5,6},{6,7},{7,8},{8,9},{9,10},{10,1... | collective-permute-start | bytes 196616 | tf_op jit(solution)/shard_map/ppermute | solution.py:16
  46.3 0.1 slice.977
  46.8 0.2 collective-permute-done.5
  47.0 0.4 fusion.32
  47.6 0.4 fusion.42
  48.3 1.3 %collective-permute-start.6 = (f32[2,1,1,64,128]{4,3,2,1,0:T(8,128)S(1)}, f32[2,1,1,64,128]{4,3,2,1,0:T(8,128)S(1)}, u32[]{:S(2)}, u32[]{:S(2)}) collective-permute-start(f32[2,1,1,64,128]{4,3,2,1,0:T(8,128)S(1)} %pad_maximum_fusion.5), channel_id=1, source_target_pairs={{1,0},{2,1},{3,2},{4,3},{5,4},{6,5},{7,6},{8,7},{9,8},{10,9},{11,1... | collective-permute-start | bytes 196616 | tf_op jit(solution)/shard_map/ppermute | solution.py:16
  49.6 1.3 %collective-permute-start.10 = (f32[2,1,1,64,128]{4,3,2,1,0:T(8,128)S(1)}, f32[2,1,1,64,128]{4,3,2,1,0:T(8,128)S(1)}, u32[]{:S(2)}, u32[]{:S(2)}) collective-permute-start(f32[2,1,1,64,128]{4,3,2,1,0:T(8,128)S(1)} %pad_maximum_fusion.9), channel_id=1, source_target_pairs={{1,0},{2,1},{3,2},{4,3},{5,4},{6,5},{7,6},{8,7},{9,8},{10,9},{11,1... | collective-permute-start | bytes 196616 | tf_op jit(solution)/shard_map/ppermute | solution.py:16
  50.9 0.5 collective-permute-done.6
  51.5 0.4 fusion.49
  51.9 1.5 %collective-permute-done.10 = f32[2,1,1,64,128]{4,3,2,1,0:T(8,128)S(1)} collective-permute-done((f32[2,1,1,64,128]{4,3,2,1,0:T(8,128)S(1)}, f32[2,1,1,64,128]{4,3,2,1,0:T(8,128)S(1)}, u32[]{:S(2)}, u32[]{:S(2)}) %collective-permute-start.10) | collective-permute-done | bytes 65568 | tf_op jit(solution)/shard_map/ppermute | solution.py:16
  53.4 0.4 fusion.115
  53.9 5.7 %collective-permute-start.11 = (f32[2,1,1,64,128]{4,3,2,1,0:T(8,128)S(1)}, f32[2,1,1,64,128]{4,3,2,1,0:T(8,128)S(1)}, u32[]{:S(2)}, u32[]{:S(2)}) collective-permute-start(f32[2,1,1,64,128]{4,3,2,1,0:T(8,128)S(1)} %pad_maximum_fusion.10), channel_id=1, source_target_pairs={{0,1},{1,2},{2,3},{3,4},{4,5},{5,6},{6,7},{7,8},{8,9},{9,10},{10,1... | collective-permute-start | bytes 196616 | tf_op jit(solution)/shard_map/ppermute | solution.py:16
  59.6 0.1 slice.917
  60.3 0.2 collective-permute-done.11
  60.5 0.2 fusion.119
  60.7 0.4 fusion.109
  61.2 1.3 %collective-permute-start.12 = (f32[2,1,1,64,128]{4,3,2,1,0:T(8,128)S(1)}, f32[2,1,1,64,128]{4,3,2,1,0:T(8,128)S(1)}, u32[]{:S(2)}, u32[]{:S(2)}) collective-permute-start(f32[2,1,1,64,128]{4,3,2,1,0:T(8,128)S(1)} %pad_maximum_fusion.11), channel_id=1, source_target_pairs={{1,0},{2,1},{3,2},{4,3},{5,4},{6,5},{7,6},{8,7},{9,8},{10,9},{11,1... | collective-permute-start | bytes 196616 | tf_op jit(solution)/shard_map/ppermute | solution.py:16
  62.5 3.0 %collective-permute-start.7 = (f32[2,1,1,64,128]{4,3,2,1,0:T(8,128)S(1)}, f32[2,1,1,64,128]{4,3,2,1,0:T(8,128)S(1)}, u32[]{:S(2)}, u32[]{:S(2)}) collective-permute-start(f32[2,1,1,64,128]{4,3,2,1,0:T(8,128)S(1)} %pad_maximum_fusion.6), channel_id=1, source_target_pairs={{0,1},{1,2},{2,3},{3,4},{4,5},{5,6},{6,7},{7,8},{8,9},{9,10},{10,1... | collective-permute-start | bytes 196616 | tf_op jit(solution)/shard_map/ppermute | solution.py:16
  66.0 0.4 fusion.126
  66.4 5.3 %collective-permute-start.13 = (f32[2,1,1,64,128]{4,3,2,1,0:T(8,128)S(1)}, f32[2,1,1,64,128]{4,3,2,1,0:T(8,128)S(1)}, u32[]{:S(2)}, u32[]{:S(2)}) collective-permute-start(f32[2,1,1,64,128]{4,3,2,1,0:T(8,128)S(1)} %pad_maximum_fusion.12), channel_id=1, source_target_pairs={{0,1},{1,2},{2,3},{3,4},{4,5},{5,6},{6,7},{7,8},{8,9},{9,10},{10,1... | collective-permute-start | bytes 196616 | tf_op jit(solution)/shard_map/ppermute | solution.py:16
  71.8 0.1 slice.1001
  72.1 0.3 collective-permute-done.13
  72.4 2.2 %fusion.156 = f32[8,64,128]{2,1,0:T(8,128)} fusion(f32[1,8,64,128]{3,2,1,0:T(8,128)S(1)} %copy-done.4, f32[1,8,64,128]{3,2,1,0:T(8,128)S(1)} %get-tuple-element.14, f32[1,8,64,128]{3,2,1,0:T(8,128)S(1)} %get-tuple-element.38, f32[1,8,63,128]{3,2,1,0:T(8,128)S(1)} %bitcast.303, f32[1,8,1,128]{3,2,1,0:T(1,128)S(1)} %slice.1015, ...), kind=kLoop, calls=%fused_computation.245 | loop fusion | flops 5111808 | bytes 11534344 | tf_op jit(solution)/shard_map/add | solution.py:80
  74.7 0.1 select_reduce_fusion
  74.8 0.7 all_to_all.9
  75.5 9.6 %all-to-all-start = ((s32[16,1,32]{2,1,0:T(1,128)}), s32[16,1,32]{2,1,0:T(1,128)S(1)}, u32[]{:S(2)}, u32[]{:S(2)}) async-start(s32[16,1,32]{2,1,0:T(1,128)} %all_to_all.9), calls=%async_computation | async-start | bytes 16384 | tf_op jit(solution)/shard_map/all_to_all | solution.py:113
  85.1 17.8 %all-reduce.6.cloned.1.call-done = f32[8,64,128]{2,1,0:T(8,128)} async-done(((f32[8,64,128]{2,1,0:T(8,128)}), f32[8,64,128]{2,1,0:T(8,128)}) %all-reduce.6.cloned.1.call-update) | async-done | bytes 262160 | tf_op jit(solution)/shard_map/psum | solution.py:83
  102.9 0.9 constant_dynamic-slice_fusion
  103.8 1.1 fusion
  105.0 5.6 %all-to-all-start.1 = ((f32[16,32,128]{2,1,0:T(8,128)}), f32[16,32,128]{2,1,0:T(8,128)S(1)}, u32[]{:S(2)}, u32[]{:S(2)}) async-start(f32[16,32,128]{2,1,0:T(8,128)} %fusion), calls=%async_computation.1 | async-start | bytes 524288 | tf_op jit(solution)/shard_map/all_to_all | solution.py:106
  110.6 0.5 broadcast.632
  111.1 0.7 reduce.5
  111.9 8.8 %all-to-all-done.1 = f32[16,32,128]{2,1,0:T(8,128)S(1)} async-done(((f32[16,32,128]{2,1,0:T(8,128)}), f32[16,32,128]{2,1,0:T(8,128)S(1)}, u32[]{:S(2)}, u32[]{:S(2)}) %all-to-all-start.1) | async-done | bytes 262176 | tf_op jit(solution)/shard_map/all_to_all | solution.py:106
  120.6 0.8 fusion.157
  (172 shorter events, 4.3 us)
Async XLA Ops:
  6.5 96.4 %all-reduce.6.cloned.1.call-start = ((), (), s32[]{:S(2)}) async-start(), calls=%async_computation.2 | async-start | bytes 524288 | tf_op jit(solution)/shard_map/psum | solution.py:83
  6.5 4.6 %collective-permute-start = (f32[2,1,1,64,128]{4,3,2,1,0:T(8,128)S(1)}, f32[2,1,1,64,128]{4,3,2,1,0:T(8,128)S(1)}, u32[]{:S(2)}, u32[]{:S(2)}) collective-permute-start(f32[2,1,1,64,128]{4,3,2,1,0:T(8,128)S(1)} %broadcast.515), channel_id=1, source_target_pairs={{1,0},{2,1},{3,2},{4,3},{5,4},{6,5},{7,6},{8,7},{9,8},{10,9},{11,1... | collective-permute-start | bytes 196616 | tf_op jit(solution)/shard_map/ppermute | solution.py:16
  8.9 0.7 copy-start.5
  10.6 0.6 copy-start.6
  11.3 4.2 %slice-start.1 = ((s32[16,3]{0,1:T(4,128)}), s32[16,2]{0,1:T(2,128)S(1)}, s32[]{:S(2)}) async-start(s32[16,3]{0,1:T(4,128)} %copy-done.6), calls=%async_computation.4 | async-start | bytes 2048 | tf_op jit(solution)/shard_map/slice.249
  11.4 5.1 %collective-permute-start.1 = (f32[2,1,1,64,128]{4,3,2,1,0:T(8,128)S(1)}, f32[2,1,1,64,128]{4,3,2,1,0:T(8,128)S(1)}, u32[]{:S(2)}, u32[]{:S(2)}) collective-permute-start(f32[2,1,1,64,128]{4,3,2,1,0:T(8,128)S(1)} %pad_maximum_fusion), channel_id=1, source_target_pairs={{0,1},{1,2},{2,3},{3,4},{4,5},{5,6},{6,7},{7,8},{8,9},{9,10},{10,1... | collective-permute-start | bytes 196616 | tf_op jit(solution)/shard_map/ppermute | solution.py:16
  15.8 1.1 copy-start.2
  15.9 1.1 copy-start
  17.8 0.7 copy-start.3
  17.8 1.2 copy-start.1
  19.7 4.3 %copy-start.4 = (f32[1,8,64,128]{3,2,1,0:T(8,128)S(1)}, f32[1,8,64,128]{3,2,1,0:T(8,128)}, u32[]{:S(2)}) copy-start(f32[1,8,64,128]{3,2,1,0:T(8,128)} %copy-done.3) | copy-start | bytes 786436
  19.8 4.3 %slice-start = ((f32[1,8,64,128]{3,2,1,0:T(8,128)}), f32[1,7,64,128]{3,2,1,0:T(8,128)S(1)}, s32[]{:S(2)}) async-start(f32[1,8,64,128]{3,2,1,0:T(8,128)} %copy-done.3), calls=%async_computation.3 | async-start | bytes 458752 | tf_op jit(solution)/shard_map/slice | solution.py:29
  19.8 4.2 %collective-permute-start.2 = (f32[2,1,1,64,128]{4,3,2,1,0:T(8,128)S(1)}, f32[2,1,1,64,128]{4,3,2,1,0:T(8,128)S(1)}, u32[]{:S(2)}, u32[]{:S(2)}) collective-permute-start(f32[2,1,1,64,128]{4,3,2,1,0:T(8,128)S(1)} %pad_maximum_fusion.1), channel_id=1, source_target_pairs={{1,0},{2,1},{3,2},{4,3},{5,4},{6,5},{7,6},{8,7},{9,8},{10,9},{11,1... | collective-permute-start | bytes 196616 | tf_op jit(solution)/shard_map/ppermute | solution.py:16
  21.3 4.7 %collective-permute-start.8 = (f32[2,1,1,64,128]{4,3,2,1,0:T(8,128)S(1)}, f32[2,1,1,64,128]{4,3,2,1,0:T(8,128)S(1)}, u32[]{:S(2)}, u32[]{:S(2)}) collective-permute-start(f32[2,1,1,64,128]{4,3,2,1,0:T(8,128)S(1)} %pad_maximum_fusion.7), channel_id=1, source_target_pairs={{1,0},{2,1},{3,2},{4,3},{5,4},{6,5},{7,6},{8,7},{9,8},{10,9},{11,1... | collective-permute-start | bytes 196616 | tf_op jit(solution)/shard_map/ppermute | solution.py:16
  26.8 7.3 %collective-permute-start.3 = (f32[2,1,1,64,128]{4,3,2,1,0:T(8,128)S(1)}, f32[2,1,1,64,128]{4,3,2,1,0:T(8,128)S(1)}, u32[]{:S(2)}, u32[]{:S(2)}) collective-permute-start(f32[2,1,1,64,128]{4,3,2,1,0:T(8,128)S(1)} %pad_maximum_fusion.2), channel_id=1, source_target_pairs={{0,1},{1,2},{2,3},{3,4},{4,5},{5,6},{6,7},{7,8},{8,9},{9,10},{10,1... | collective-permute-start | bytes 196616 | tf_op jit(solution)/shard_map/ppermute | solution.py:16
  32.2 4.0 %collective-permute-start.9 = (f32[2,1,1,64,128]{4,3,2,1,0:T(8,128)S(1)}, f32[2,1,1,64,128]{4,3,2,1,0:T(8,128)S(1)}, u32[]{:S(2)}, u32[]{:S(2)}) collective-permute-start(f32[2,1,1,64,128]{4,3,2,1,0:T(8,128)S(1)} %pad_maximum_fusion.8), channel_id=1, source_target_pairs={{0,1},{1,2},{2,3},{3,4},{4,5},{5,6},{6,7},{7,8},{8,9},{9,10},{10,1... | collective-permute-start | bytes 196616 | tf_op jit(solution)/shard_map/ppermute | solution.py:16
  34.8 6.0 %collective-permute-start.4 = (f32[2,1,1,64,128]{4,3,2,1,0:T(8,128)S(1)}, f32[2,1,1,64,128]{4,3,2,1,0:T(8,128)S(1)}, u32[]{:S(2)}, u32[]{:S(2)}) collective-permute-start(f32[2,1,1,64,128]{4,3,2,1,0:T(8,128)S(1)} %pad_maximum_fusion.3), channel_id=1, source_target_pairs={{1,0},{2,1},{3,2},{4,3},{5,4},{6,5},{7,6},{8,7},{9,8},{10,9},{11,1... | collective-permute-start | bytes 196616 | tf_op jit(solution)/shard_map/ppermute | solution.py:16
  41.3 5.7 %collective-permute-start.5 = (f32[2,1,1,64,128]{4,3,2,1,0:T(8,128)S(1)}, f32[2,1,1,64,128]{4,3,2,1,0:T(8,128)S(1)}, u32[]{:S(2)}, u32[]{:S(2)}) collective-permute-start(f32[2,1,1,64,128]{4,3,2,1,0:T(8,128)S(1)} %pad_maximum_fusion.4), channel_id=1, source_target_pairs={{0,1},{1,2},{2,3},{3,4},{4,5},{5,6},{6,7},{7,8},{8,9},{9,10},{10,1... | collective-permute-start | bytes 196616 | tf_op jit(solution)/shard_map/ppermute | solution.py:16
  48.3 3.1 %collective-permute-start.6 = (f32[2,1,1,64,128]{4,3,2,1,0:T(8,128)S(1)}, f32[2,1,1,64,128]{4,3,2,1,0:T(8,128)S(1)}, u32[]{:S(2)}, u32[]{:S(2)}) collective-permute-start(f32[2,1,1,64,128]{4,3,2,1,0:T(8,128)S(1)} %pad_maximum_fusion.5), channel_id=1, source_target_pairs={{1,0},{2,1},{3,2},{4,3},{5,4},{6,5},{7,6},{8,7},{9,8},{10,9},{11,1... | collective-permute-start | bytes 196616 | tf_op jit(solution)/shard_map/ppermute | solution.py:16
  49.6 3.8 %collective-permute-start.10 = (f32[2,1,1,64,128]{4,3,2,1,0:T(8,128)S(1)}, f32[2,1,1,64,128]{4,3,2,1,0:T(8,128)S(1)}, u32[]{:S(2)}, u32[]{:S(2)}) collective-permute-start(f32[2,1,1,64,128]{4,3,2,1,0:T(8,128)S(1)} %pad_maximum_fusion.9), channel_id=1, source_target_pairs={{1,0},{2,1},{3,2},{4,3},{5,4},{6,5},{7,6},{8,7},{9,8},{10,9},{11,1... | collective-permute-start | bytes 196616 | tf_op jit(solution)/shard_map/ppermute | solution.py:16
  53.9 6.6 %collective-permute-start.11 = (f32[2,1,1,64,128]{4,3,2,1,0:T(8,128)S(1)}, f32[2,1,1,64,128]{4,3,2,1,0:T(8,128)S(1)}, u32[]{:S(2)}, u32[]{:S(2)}) collective-permute-start(f32[2,1,1,64,128]{4,3,2,1,0:T(8,128)S(1)} %pad_maximum_fusion.10), channel_id=1, source_target_pairs={{0,1},{1,2},{2,3},{3,4},{4,5},{5,6},{6,7},{7,8},{8,9},{9,10},{10,1... | collective-permute-start | bytes 196616 | tf_op jit(solution)/shard_map/ppermute | solution.py:16
  61.2 4.8 %collective-permute-start.12 = (f32[2,1,1,64,128]{4,3,2,1,0:T(8,128)S(1)}, f32[2,1,1,64,128]{4,3,2,1,0:T(8,128)S(1)}, u32[]{:S(2)}, u32[]{:S(2)}) collective-permute-start(f32[2,1,1,64,128]{4,3,2,1,0:T(8,128)S(1)} %pad_maximum_fusion.11), channel_id=1, source_target_pairs={{1,0},{2,1},{3,2},{4,3},{5,4},{6,5},{7,6},{8,7},{9,8},{10,9},{11,1... | collective-permute-start | bytes 196616 | tf_op jit(solution)/shard_map/ppermute | solution.py:16
  62.5 9.2 %collective-permute-start.7 = (f32[2,1,1,64,128]{4,3,2,1,0:T(8,128)S(1)}, f32[2,1,1,64,128]{4,3,2,1,0:T(8,128)S(1)}, u32[]{:S(2)}, u32[]{:S(2)}) collective-permute-start(f32[2,1,1,64,128]{4,3,2,1,0:T(8,128)S(1)} %pad_maximum_fusion.6), channel_id=1, source_target_pairs={{0,1},{1,2},{2,3},{3,4},{4,5},{5,6},{6,7},{7,8},{8,9},{9,10},{10,1... | collective-permute-start | bytes 196616 | tf_op jit(solution)/shard_map/ppermute | solution.py:16
  66.4 6.0 %collective-permute-start.13 = (f32[2,1,1,64,128]{4,3,2,1,0:T(8,128)S(1)}, f32[2,1,1,64,128]{4,3,2,1,0:T(8,128)S(1)}, u32[]{:S(2)}, u32[]{:S(2)}) collective-permute-start(f32[2,1,1,64,128]{4,3,2,1,0:T(8,128)S(1)} %pad_maximum_fusion.12), channel_id=1, source_target_pairs={{0,1},{1,2},{2,3},{3,4},{4,5},{5,6},{6,7},{7,8},{8,9},{9,10},{10,1... | collective-permute-start | bytes 196616 | tf_op jit(solution)/shard_map/ppermute | solution.py:16
  75.5 29.5 %all-to-all-start = ((s32[16,1,32]{2,1,0:T(1,128)}), s32[16,1,32]{2,1,0:T(1,128)S(1)}, u32[]{:S(2)}, u32[]{:S(2)}) async-start(s32[16,1,32]{2,1,0:T(1,128)} %all_to_all.9), calls=%async_computation | async-start | bytes 16384 | tf_op jit(solution)/shard_map/all_to_all | solution.py:113
  105.0 15.7 %all-to-all-start.1 = ((f32[16,32,128]{2,1,0:T(8,128)}), f32[16,32,128]{2,1,0:T(8,128)S(1)}, u32[]{:S(2)}, u32[]{:S(2)}) async-start(f32[16,32,128]{2,1,0:T(8,128)} %fusion), calls=%async_computation.1 | async-start | bytes 524288 | tf_op jit(solution)/shard_map/all_to_all | solution.py:106
Sparse Core Ops, SparseCore 0:
  74.8 28.0 all-reduce.5
where the time goes:
time: 129 us; the launch traced here: 128 us
  starting transfers between devices  54.8 us (42%)
  waiting for transfers between devices  36.2 us (28%)
  between operations  16.1 us (12%)
  other arithmetic  9.71 us (8%)
  local copies, waits for them, and re-layouts  9.63 us (7%)
  matrix products  1.94 us (2%)
    ppermute x14, starting transfers between devices, passed_along(): return lax.ppermute(block, axis, route)  39.5 us
    psum x1, waiting for transfers between devices, per_device(): summed = lax.psum(local_grad, 'src')  17.8 us
    ppermute x14, waiting for transfers between devices, passed_along(): return lax.ppermute(block, axis, route)  9.62 us
    all_to_all x1, starting transfers between devices, per_device(): lax.all_to_all(packed_ids.reshape(owners, capacity), 'space', split_axis=...  9.6 us
    all_to_all x1, waiting for transfers between devices, per_device(): lax.all_to_all(packed.reshape(owners, capacity, depth), 'space', split_ax...  8.78 us
    all_to_all x1, starting transfers between devices, per_device(): lax.all_to_all(packed.reshape(owners, capacity, depth), 'space', split_ax...  5.62 us
    unnamed x14, local copies, waits for them, and re-layouts  2.77 us
  transfers between devices with their start and end apart: 17, of which 11 were waited for; matrix products, arithmetic and copies ran while one was open for 8% of the time, Pallas kernels for 0%

commit v1 on v0

v1 whole, which is shorter than its diff:
```python
import functools

import jax
import jax.numpy as jnp
from jax import lax
from jax.experimental import pallas as pl
from jax.experimental.pallas import tpu as pltpu
from jax.sharding import PartitionSpec as P

ITERS = 4
PIX_DEV = 16
PIECES = ((3, 2), (0, 3), (5, 3))
MESH = pl.DeviceIdType.MESH


def ahead(f, axis):
    return pltpu.roll(f, f.shape[axis] - 1, axis)


def behind(f, axis):
    return pltpu.roll(f, 1, axis)


def next_h(h, e, e_next):
    e1, e2, e3 = e
    x2 = -e2 if e_next is None else e_next[0] - e2
    x3 = -e3 if e_next is None else e_next[1] - e3
    curl = (
        (ahead(e3, 0) - e3) - (ahead(e2, 1) - e2),
        (ahead(e1, 1) - e1) - x3,
        x2 - (ahead(e1, 0) - e1),
    )
    if h is None:
        return tuple(-v for v in curl)
    return tuple(a - v for a, v in zip(h, curl))


def curl_h(h, h_prev):
    h1, h2, h3 = h
    x2 = h2 if h_prev is None else h2 - h_prev[0]
    x3 = h3 if h_prev is None else h3 - h_prev[1]
    return (
        (h3 - behind(h3, 0)) - (h2 - behind(h2, 1)),
        (h1 - behind(h1, 1)) - x3,
        x2 - (h1 - behind(h1, 0)),
    )


def kernel(n, nsrc, fwd, adj, eps, wave, foot, out,
           J, C, E, H, HI, EL, EH, send_e, send_h, recv_e, recv_h, c_lo, c_hi,
           lo_h, lo_e, hi_e, sig, G, R, T, RT,
           load_sem, es_sem, er_sem, hs_sem, hr_sem, gs_sem, gr_sem, ts_sem, tr_sem):
    me = lax.axis_index("space")
    src = lax.axis_index("src")
    low, high = lax.rem(me + n - 1, n), lax.rem(me + 1, n)
    has_low, has_high = me > 0, me < n - 1
    ys = G.shape[2]

    loads = [
        pltpu.make_async_copy(eps, C, load_sem.at[0]),
        pltpu.make_async_copy(fwd.at[0], J.at[0], load_sem.at[1]),
        pltpu.make_async_copy(adj.at[0], J.at[1], load_sem.at[2]),
    ]
    for copy in loads:
        copy.start()

    barrier = pltpu.get_barrier_semaphore()
    for d in range(1, n):
        pl.semaphore_signal(barrier, inc=1, device_id={"space": lax.rem(me + d, n)}, device_id_type=MESH)
    for d in range(1, nsrc):
        pl.semaphore_signal(barrier, inc=1, device_id={"src": lax.rem(src + d, nsrc)}, device_id_type=MESH)

    omega = 0.25 + 0.05 * wave[0].astype(jnp.float32)
    when = (lax.broadcasted_iota(jnp.int32, (8, 128), 0) + 1).astype(jnp.float32)
    sig[0] = jnp.sin(omega * when)
    sig[1] = jnp.cos(omega * when)

    def remote(a, b, s, r, where):
        return pltpu.make_async_remote_copy(
            src_ref=a, dst_ref=b, send_sem=s, recv_sem=r, device_id=where, device_id_type=MESH)

    e_copies = [remote(send_e.at[t], recv_e.at[t], es_sem.at[t], er_sem.at[t], {"space": low}) for t in range(3)]
    e_copies.append(remote(eps.at[0], c_hi, es_sem.at[3], er_sem.at[3], {"space": low}))
    h_copies = [remote(send_h.at[t], recv_h.at[t], hs_sem.at[t], hr_sem.at[t], {"space": high}) for t in range(3)]
    h_copies.append(remote(eps.at[7], c_lo, hs_sem.at[3], hr_sem.at[3], {"space": high}))

    def start_e(t):
        pl.when(has_low)(lambda: e_copies[t].start())

    def start_h(t):
        pl.when(has_high)(lambda: h_copies[t].start())

    def arrived(t):
        pl.when(has_low)(lambda: h_copies[t].wait_recv())
        pl.when(has_high)(lambda: e_copies[t].wait_recv())

    @pl.when(jnp.logical_not(has_low))
    def _():
        recv_h[...] = jnp.zeros_like(recv_h)
        c_lo[...] = jnp.zeros_like(c_lo)

    @pl.when(jnp.logical_not(has_high))
    def _():
        recv_e[...] = jnp.zeros_like(recv_e)
        c_hi[...] = jnp.zeros_like(c_hi)

    m_lo = jnp.where(has_low, 1.0, 0.0).astype(jnp.float32)
    m_hi = jnp.where(has_high, 1.0, 0.0).astype(jnp.float32)

    def get(ref, *at):
        return tuple(ref[(*at[:-1], k, at[-1])] for k in range(3))

    def put(ref, vals, *at):
        for k in range(3):
            ref[(*at[:-1], k, at[-1])] = vals[k]

    def get3(ref, r):
        return tuple(ref[r, k] for k in range(3))

    def put3(ref, r, vals):
        for k in range(3):
            ref[r, k] = vals[k]

    def pair(ref, t, r):
        return ref[t, r, 0], ref[t, r, 1]

    def put_pair(ref, t, r, vals):
        ref[t, r, 0], ref[t, r, 1] = vals[1], vals[2]

    def e_at(t, r, p):
        return tuple(E[t, r, k, p] for k in range(3))

    def step_e(t, r, p, e, h, h_prev):
        c, s = C[p], sig[r, t:t + 1, :]
        curl = curl_h(h, h_prev)
        return tuple(e[k] + c * curl[k] - s * J[r, k, p] for k in range(3))

    def do_h(t, r, p):
        e, nxt = e_at(t, r, p), (E[t, r, 1, p + 1], E[t, r, 2, p + 1])
        put(H, next_h(None if t == 0 else get(H, r, p), e, nxt), r, p)

    def do_e(t, r, p):
        new = step_e(t, r, p, e_at(t - 1, r, p), get(H, r, p), (H[r, 1, p - 1], H[r, 2, p - 1]))
        for k in range(3):
            E[t, r, k, p] = new[k]

    def put_e(t, r, p, new):
        for k in range(3):
            E[t, r, k, p] = new[k]

    def runs(body):
        lax.fori_loop(0, 2, lambda r, _: (body(r), 0)[1], 0)

    def planes(first, last, body):
        count = last - first

        def one(i, _):
            body(i // count, first + i % count)
            return 0

        lax.fori_loop(0, 2 * count, one, 0)

    def begin(r, p):
        c2, s = 2.0 * C[p], sig[r, 0:1, :]
        for k in range(3):
            a = c2 * J[r, k, p]
            J[r, k, p] = a
            E[0, r, k, p] = -s * a

    pl.semaphore_wait(barrier, n - 1 + nsrc - 1)
    start_e(3)
    start_h(3)
    for copy in loads:
        copy.wait()

    def scale(p, _):
        C[p] = 0.25 * C[p]
        return 0

    lax.fori_loop(0, 8, scale, 0)

    def first(r):
        begin(r, 0)
        put_pair(send_e, 0, r, e_at(0, r, 0))
        begin(r, 7)
        h = next_h(None, e_at(0, r, 7), None)
        put3(HI, r, h)
        put_pair(send_h, 0, r, h)

    runs(first)
    start_e(0)
    start_h(0)
    planes(1, 7, begin)
    planes(0, 7, functools.partial(do_h, 0))

    def second(r):
        e = step_e(1, r, 0, e_at(0, r, 0), get(H, r, 0), None)
        put3(EL, r, e)
        put_pair(send_e, 1, r, e)

    runs(second)
    start_e(1)

    def third(r):
        do_e(1, r, 6)
        h7 = get3(HI, r)
        e7 = step_e(1, r, 7, e_at(0, r, 7), h7, (H[r, 1, 6], H[r, 2, 6]))
        put3(EH, r, e7)
        h7 = next_h(h7, e7, None)
        put3(HI, r, h7)
        put_pair(send_h, 1, r, h7)

    runs(third)
    start_h(1)

    def fourth(r):
        do_e(1, r, 1)
        e = get3(EL, r)
        h = next_h(get(H, r, 0), e, (E[1, r, 1, 1], E[1, r, 2, 1]))
        put_pair(send_e, 2, r, step_e(2, r, 0, e, h, None))

    runs(fourth)
    start_e(2)

    def fifth(r):
        e7, h7 = get3(EH, r), get3(HI, r)
        h6 = next_h(get(H, r, 6), e_at(1, r, 6), (e7[1], e7[2]))
        e7 = step_e(2, r, 7, e7, h7, (h6[1], h6[2]))
        put_pair(send_h, 2, r, next_h(h7, e7, None))

    runs(fifth)
    start_h(2)

    planes(2, 6, functools.partial(do_e, 1))
    planes(1, 6, functools.partial(do_h, 1))
    planes(2, 6, functools.partial(do_e, 2))
    planes(2, 5, functools.partial(do_h, 2))
    planes(3, 5, functools.partial(do_e, 3))

    def product(p):
        total = None
        for t in range(ITERS):
            for k in range(3):
                term = E[t, 0, k, p] * E[ITERS - 1 - t, 1, k, p]
                total = term if total is None else total + term
        for j in range(nsrc):
            G[j, p] = total[j * ys:(j + 1) * ys]

    def products(a, b):
        lax.fori_loop(a, b, lambda p, _: (product(p), 0)[1], 0)

    g_copies = []
    for piece, (start, size) in enumerate(PIECES):
        g_copies.append([
            remote(G.at[lax.rem(src + d, nsrc), pl.ds(start, size)], R.at[d - 1, pl.ds(start, size)],
                   gs_sem.at[d - 1, piece], gr_sem.at[d - 1, piece], {"src": lax.rem(src + d, nsrc)})
            for d in range(1, nsrc)
        ])

    def start_g(piece):
        for copy in g_copies[piece]:
            copy.start()

    products(3, 5)
    start_g(0)

    arrived(3)
    arrived(0)

    def step2(r):
        e0 = e_at(0, r, 0)
        d2, d3 = m_lo * e0[2], -m_lo * e0[1]
        zero = jnp.zeros_like(d2)
        h = pair(recv_h, 0, r)
        put_e(1, r, 0, step_e(1, r, 0, e0, get(H, r, 0), (h[0] + d2, h[1] + d3)))
        put3(lo_h, r, (zero, d2, d3))
        c = 0.25 * c_lo[...]
        put3(lo_e, r, tuple(c * v for v in curl_h((zero, d2, d3), None)))
        e7 = e_at(0, r, 7)
        h7 = next_h(None, e7, pair(recv_e, 0, r))
        put(H, h7, r, 7)
        put_e(1, r, 7, step_e(1, r, 7, e7, h7, (H[r, 1, 6], H[r, 2, 6])))
        c = m_hi * 0.25 * c_hi[...]
        put3(hi_e, r, (zero, c * h7[2], -c * h7[1]))

    runs(step2)
    arrived(1)

    def step3(r):
        do_h(1, r, 0)
        e0 = e_at(1, r, 0)
        de = get3(lo_e, r)
        dh = next_h(get3(lo_h, r), de, (m_lo * e0[1], m_lo * e0[2]))
        put3(lo_h, r, dh)
        h = pair(recv_h, 1, r)
        put_e(2, r, 0, step_e(2, r, 0, e0, get(H, r, 0), (h[0] + dh[1], h[1] + dh[2])))
        c = 0.25 * c_lo[...]
        curl = curl_h(dh, (de[2], -de[1]))
        put3(lo_e, r, tuple(de[k] + c * curl[k] for k in range(3)))
        do_e(2, r, 1)
        do_h(1, r, 6)
        de = get3(hi_e, r)
        e = pair(recv_e, 1, r)
        h7 = next_h(get(H, r, 7), e_at(1, r, 7), (e[0] + de[1], e[1] + de[2]))
        put(H, h7, r, 7)
        do_e(2, r, 7)
        do_e(2, r, 6)
        c = 0.25 * c_hi[...]
        curl = curl_h(next_h(None, de, None), (m_hi * h7[1], m_hi * h7[2]))
        put3(hi_e, r, tuple(de[k] + c * curl[k] for k in range(3)))

    runs(step3)
    arrived(2)

    def low4(r):
        e0 = e_at(2, r, 0)
        dh = next_h(get3(lo_h, r), get3(lo_e, r), (m_lo * e0[1], m_lo * e0[2]))
        h = pair(recv_h, 2, r)
        do_h(2, r, 0)
        do_h(2, r, 1)
        put_e(3, r, 0, step_e(3, r, 0, e0, get(H, r, 0), (h[0] + dh[1], h[1] + dh[2])))
        do_e(3, r, 1)
        do_e(3, r, 2)

    runs(low4)
    products(0, 3)
    start_g(1)

    def high4(r):
        de = get3(hi_e, r)
        e = pair(recv_e, 2, r)
        put(H, next_h(get(H, r, 7), e_at(2, r, 7), (e[0] + de[1], e[1] + de[2])), r, 7)
        do_h(2, r, 6)
        do_h(2, r, 5)
        do_e(3, r, 7)
        do_e(3, r, 6)
        do_e(3, r, 5)

    runs(high4)
    products(5, 8)
    start_g(2)

    pixels = n * PIX_DEV
    ids = foot[...] - src * pixels
    row = lax.broadcasted_iota(jnp.int32, (pixels, ys), 0)
    chosen = [(row == ids[p:p + 1, :]).astype(jnp.float32).astype(jnp.bfloat16) for p in range(8)]
    total = jnp.zeros((pixels, 128), jnp.float32)
    for piece, (start, size) in enumerate(PIECES):
        for copy in g_copies[piece]:
            copy.wait_recv()
        for p in range(start, start + size):
            block = G[src, p]
            for d in range(1, nsrc):
                block = block + R[d - 1, p]
            head = block.astype(jnp.bfloat16)
            tail = (block - head.astype(jnp.float32)).astype(jnp.bfloat16)
            total = total + jnp.dot(chosen[p], head, preferred_element_type=jnp.float32)
            total = total + jnp.dot(chosen[p], tail, preferred_element_type=jnp.float32)
    T[...] = total.reshape(n, PIX_DEV, 128)

    t_copies = [
        remote(T.at[lax.rem(me + d, n)], RT.at[d - 1], ts_sem.at[d - 1], tr_sem.at[d - 1],
               {"space": lax.rem(me + d, n)})
        for d in range(1, n)
    ]
    for copy in t_copies:
        copy.start()
    result = T[me]
    for d in range(1, n):
        t_copies[d - 1].wait_recv()
        result = result + RT[d - 1]
    out[...] = result

    for copy in t_copies:
        copy.wait_send()
    for piece in g_copies:
        for copy in piece:
            copy.wait_send()
    for t in range(4):
        pl.when(has_low)(lambda: e_copies[t].wait_send())
        pl.when(has_high)(lambda: h_copies[t].wait_send())


def solution(mesh):
    n, nsrc = mesh.shape["space"], mesh.shape["src"]

    def per_device(fwd, adj, eps, wave, foot):
        cx, ny, nz = eps.shape
        ys = foot.shape[1]
        f32 = jnp.float32
        plane = (ny, nz)

        def vmem(*shape):
            return pltpu.VMEM(shape, f32)

        dma = pltpu.SemaphoreType.DMA
        any_spec = pl.BlockSpec(memory_space=pl.ANY)
        return pl.pallas_call(
            functools.partial(kernel, n, nsrc),
            out_shape=jax.ShapeDtypeStruct((PIX_DEV, nz), f32),
            in_specs=[any_spec, any_spec, any_spec, pl.BlockSpec(memory_space=pltpu.SMEM),
                      pl.BlockSpec(memory_space=pltpu.VMEM)],
            out_specs=pl.BlockSpec(memory_space=pltpu.VMEM),
            scratch_shapes=[
                vmem(2, 3, cx, *plane), vmem(cx, *plane), vmem(ITERS, 2, 3, cx, *plane),
                vmem(2, 3, cx, *plane), vmem(2, 3, *plane), vmem(2, 3, *plane), vmem(2, 3, *plane),
                vmem(3, 2, 2, *plane), vmem(3, 2, 2, *plane), vmem(3, 2, 2, *plane), vmem(3, 2, 2, *plane),
                vmem(*plane), vmem(*plane),
                vmem(2, 3, *plane), vmem(2, 3, *plane), vmem(2, 3, *plane), vmem(2, 8, 128),
                vmem(nsrc, cx, ys, nz), vmem(nsrc - 1, cx, ys, nz),
                vmem(n, PIX_DEV, nz), vmem(n - 1, PIX_DEV, nz),
                dma((3,)), dma((4,)), dma((4,)), dma((4,)), dma((4,)),
                dma((nsrc - 1, 3)), dma((nsrc - 1, 3)), dma((n - 1,)), dma((n - 1,)),
            ],
            compiler_params=pltpu.CompilerParams(
                collective_id=0, has_side_effects=True, vmem_limit_bytes=40 * 1024 * 1024),
            cost_estimate=pl.CostEstimate(flops=30_000_000, bytes_accessed=2_000_000, transcendentals=0),
        )(fwd, adj, eps, wave, foot)

    in_specs = (
        P("src", None, "space", None, None),
        P("src", None, "space", None, None),
        P("space", None, None),
        P("src"),
        P("space", "src"),
    )
    return jax.shard_map(
        per_device, mesh=mesh, in_specs=in_specs, out_specs=P(("src", "space"), None), check_vma=False)
```

time: 129 us -> 31.2 us (0.24)
  starting transfers between devices: 54.8 us -> 0 us
  waiting for transfers between devices: 36.2 us -> 0 us
  Pallas kernels: 0 us -> 25.8 us
  between operations: 16.1 us -> 0.67 us
  other arithmetic: 9.71 us -> 0 us
  local copies, waits for them, and re-layouts: 9.63 us -> 4.5 us
  matrix products: 1.94 us -> 0 us
    ppermute x14 -> x0, starting transfers between devices: 39.5 us -> none  [passed_along(): return lax.ppermute(block, axis, route)]
    pallas_call x0 -> x1, Pallas kernels: none -> 25.8 us  [per_device(): pl.pallas_call(functools.partial(kernel, n, nsrc), out_shape=jax.ShapeDty...]
    psum x1 -> x0, waiting for transfers between devices: 17.8 us -> none  [per_device(): summed = lax.psum(local_grad, 'src')]
    all_to_all x2 -> x0, starting transfers between devices: 15.2 us -> none  [the longest x1 9.6 us: per_device(): lax.all_to_all(packed_ids.reshape(owners, capacity), 'space', split_axis=...]
    ppermute x14 -> x0, waiting for transfers between devices: 9.62 us -> none  [passed_along(): return lax.ppermute(block, axis, route)]
    all_to_all x2 -> x0, waiting for transfers between devices: 8.78 us -> none  [the longest x1 8.78 us: per_device(): lax.all_to_all(packed.reshape(owners, capacity, depth), 'space', split_ax...]
    add x9 -> x0, other arithmetic: 4.74 us -> none  [the longest x7 2.54 us: run_fields(): electric[k] + COURANT * inv_eps[None] * (curl_h[k] - current[:, k] * signal)]
    slice x93 -> x0, local copies, waits for them, and re-layouts: 4.11 us -> none  [the longest x28 1.84 us: roll_back(): return field - jnp.roll(field, 1, axis)]
  transfers between devices with their start and end apart: 17 -> 0, of which waited for: 11 -> 0; matrix products, arithmetic and copies ran while one was open for 8% -> 0% of each run, Pallas kernels for 0% -> 0%
where the time goes in v1:
time: 31.2 us; the launch traced here: 30.9 us
  Pallas kernels  25.8 us (83%)
  local copies, waits for them, and re-layouts  4.5 us (14%)
  between operations  0.67 us (2%)
    pallas_call x1, Pallas kernels, per_device(): pl.pallas_call(functools.partial(kernel, n, nsrc), out_shape=jax.ShapeDty...  25.8 us
    unnamed x9, local copies, waits for them, and re-layouts  4.5 us

profile of v1, /device:TPU:0, one launch (start us, length us, event | category | flops | bytes accessed | tf_op | source)
XLA Modules:
  0.0 30.9 jit_solution(12559238922161845995)
XLA Ops:
  0.7 0.0 copy-start
  0.7 1.1 %copy-done = f32[1,3,8,64,128]{4,3,2,1,0:T(8,128)S(1)} copy-done((f32[1,3,8,64,128]{4,3,2,1,0:T(8,128)S(1)}, f32[1,3,8,64,128]{4,3,2,1,0:T(8,128)}, u32[]{:S(2)}) %copy-start) | copy-done | bytes 786456
  1.8 0.0 copy-start.1
  1.8 1.1 %copy-done.1 = f32[1,3,8,64,128]{4,3,2,1,0:T(8,128)S(1)} copy-done((f32[1,3,8,64,128]{4,3,2,1,0:T(8,128)S(1)}, f32[1,3,8,64,128]{4,3,2,1,0:T(8,128)}, u32[]{:S(2)}) %copy-start.1) | copy-done | bytes 786456
  2.9 0.0 copy-start.2
  2.9 0.9 %copy-done.2 = f32[8,64,128]{2,1,0:T(8,128)S(1)} copy-done((f32[8,64,128]{2,1,0:T(8,128)S(1)}, f32[8,64,128]{2,1,0:T(8,128)}, u32[]{:S(2)}) %copy-start.2) | copy-done | bytes 262168
  3.9 0.0 copy-start.3
  3.9 0.7 %copy-done.3 = s32[8,32]{1,0:T(8,128)S(1)} copy-done((s32[8,32]{1,0:T(8,128)S(1)}, s32[8,32]{1,0:T(8,128)}, u32[]{:S(2)}) %copy-start.3) | copy-done | bytes 1048
  4.6 25.8 %shard_map.55 = f32[16,128]{1,0:T(8,128)S(1)} custom-call(f32[1,3,8,64,128]{4,3,2,1,0:T(8,128)S(1)} %copy-done, f32[1,3,8,64,128]{4,3,2,1,0:T(8,128)S(1)} %copy-done.1, f32[8,64,128]{2,1,0:T(8,128)S(1)} %copy-done.2, s32[1]{0:T(128)S(6)} %copy.7.wave, s32[8,32]{1,0:T(8,128)S(1)} %copy-done.3), custom_call_target="tpu_custom_call" | custom-call | flops 30000000 | bytes 2000000 | tf_op jit(solution)/shard_map/pallas_call | solution.py:398
  30.3 0.6 %copy.8 = f32[16,128]{1,0:T(8,128)} copy(f32[16,128]{1,0:T(8,128)S(1)} %shard_map.55) | data formatting | bytes 16384
Async XLA Ops:
  0.7 1.1 %copy-start = (f32[1,3,8,64,128]{4,3,2,1,0:T(8,128)S(1)}, f32[1,3,8,64,128]{4,3,2,1,0:T(8,128)}, u32[]{:S(2)}) copy-start(f32[1,3,8,64,128]{4,3,2,1,0:T(8,128)} %fwd.1) | copy-start | bytes 2359300
  1.8 1.1 %copy-start.1 = (f32[1,3,8,64,128]{4,3,2,1,0:T(8,128)S(1)}, f32[1,3,8,64,128]{4,3,2,1,0:T(8,128)}, u32[]{:S(2)}) copy-start(f32[1,3,8,64,128]{4,3,2,1,0:T(8,128)} %adj.1) | copy-start | bytes 2359300
  2.9 0.9 %copy-start.2 = (f32[8,64,128]{2,1,0:T(8,128)S(1)}, f32[8,64,128]{2,1,0:T(8,128)}, u32[]{:S(2)}) copy-start(f32[8,64,128]{2,1,0:T(8,128)} %eps.1) | copy-start | bytes 786436
  3.9 0.7 %copy-start.3 = (s32[8,32]{1,0:T(8,128)S(1)}, s32[8,32]{1,0:T(8,128)}, u32[]{:S(2)}) copy-start(s32[8,32]{1,0:T(8,128)} %foot.1) | copy-start | bytes 3076

commit v2 on v1

--- a/solution.py
+++ b/solution.py
@@ -14,11 +14,20 @@
 
 
 def ahead(f, axis):
-    return pltpu.roll(f, f.shape[axis] - 1, axis)
+    if axis == 1:
+        return pltpu.roll(f, f.shape[2] - 1, 2)
+    return jnp.concatenate([f[1:], pltpu.roll(f[:1], 7, 1)], axis=0)
 
 
 def behind(f, axis):
-    return pltpu.roll(f, 1, axis)
+    if axis == 1:
+        return pltpu.roll(f, 1, 2)
+    return jnp.concatenate([pltpu.roll(f[-1:], 1, 1), f[:-1]], axis=0)
+
+
+def dealt(ref, *at):
+    folds = ref.shape[-2] // 8
+    return jnp.stack([ref[(*at, pl.ds(j, 8, stride=folds), slice(None))] for j in range(folds)])
 
 
 def next_h(h, e, e_next):
@@ -46,20 +55,21 @@
     )
 
 
-def kernel(n, nsrc, fwd, adj, eps, wave, foot, out,
-           J, C, E, H, HI, EL, EH, send_e, send_h, recv_e, recv_h, c_lo, c_hi,
+def kernel(n, nsrc, fwd, adj, eps, wave, foot_hbm, out,
+           foot, JR, CR, J, C, E, H, HI, EL, EH, send_e, send_h, recv_e, recv_h, c_lo, c_hi,
            lo_h, lo_e, hi_e, sig, G, R, T, RT,
            load_sem, es_sem, er_sem, hs_sem, hr_sem, gs_sem, gr_sem, ts_sem, tr_sem):
     me = lax.axis_index("space")
     src = lax.axis_index("src")
     low, high = lax.rem(me + n - 1, n), lax.rem(me + 1, n)
     has_low, has_high = me > 0, me < n - 1
-    ys = G.shape[2]
+    ys = foot.shape[1]
 
     loads = [
-        pltpu.make_async_copy(eps, C, load_sem.at[0]),
-        pltpu.make_async_copy(fwd.at[0], J.at[0], load_sem.at[1]),
-        pltpu.make_async_copy(adj.at[0], J.at[1], load_sem.at[2]),
+        pltpu.make_async_copy(eps, CR, load_sem.at[0]),
+        pltpu.make_async_copy(fwd.at[0], JR.at[0], load_sem.at[1]),
+        pltpu.make_async_copy(adj.at[0], JR.at[1], load_sem.at[2]),
+        pltpu.make_async_copy(foot_hbm, foot, load_sem.at[3]),
     ]
     for copy in loads:
         copy.start()
@@ -152,29 +162,25 @@
         lax.fori_loop(0, 2, lambda r, _: (body(r), 0)[1], 0)
 
     def planes(first, last, body):
-        count = last - first
-
-        def one(i, _):
-            body(i // count, first + i % count)
+        def one(p, _):
+            body(0, p)
+            body(1, p)
             return 0
 
-        lax.fori_loop(0, 2 * count, one, 0)
+        lax.fori_loop(first, last, one, 0)
 
     def begin(r, p):
         c2, s = 2.0 * C[p], sig[r, 0:1, :]
         for k in range(3):
-            a = c2 * J[r, k, p]
+            a = c2 * dealt(JR, r, k, p)
             J[r, k, p] = a
             E[0, r, k, p] = -s * a
 
-    pl.semaphore_wait(barrier, n - 1 + nsrc - 1)
-    start_e(3)
-    start_h(3)
     for copy in loads:
         copy.wait()
 
     def scale(p, _):
-        C[p] = 0.25 * C[p]
+        C[p] = 0.25 * dealt(CR, p)
         return 0
 
     lax.fori_loop(0, 8, scale, 0)
@@ -188,6 +194,9 @@
         put_pair(send_h, 0, r, h)
 
     runs(first)
+    pl.semaphore_wait(barrier, n - 1 + nsrc - 1)
+    start_e(3)
+    start_h(3)
     start_e(0)
     start_h(0)
     planes(1, 7, begin)
@@ -243,16 +252,20 @@
             for k in range(3):
                 term = E[t, 0, k, p] * E[ITERS - 1 - t, 1, k, p]
                 total = term if total is None else total + term
-        for j in range(nsrc):
-            G[j, p] = total[j * ys:(j + 1) * ys]
+        folds = total.shape[0]
+        for j in range(folds):
+            G[p, pl.ds(j, 8, stride=folds), :] = total[j]
 
     def products(a, b):
         lax.fori_loop(a, b, lambda p, _: (product(p), 0)[1], 0)
+
+    def share(j):
+        return pl.ds(pl.multiple_of(j * ys, 8), ys)
 
     g_copies = []
     for piece, (start, size) in enumerate(PIECES):
         g_copies.append([
-            remote(G.at[lax.rem(src + d, nsrc), pl.ds(start, size)], R.at[d - 1, pl.ds(start, size)],
+            remote(G.at[pl.ds(start, size), share(lax.rem(src + d, nsrc))], R.at[d - 1, pl.ds(start, size)],
                    gs_sem.at[d - 1, piece], gr_sem.at[d - 1, piece], {"src": lax.rem(src + d, nsrc)})
             for d in range(1, nsrc)
         ])
@@ -274,13 +287,13 @@
         h = pair(recv_h, 0, r)
         put_e(1, r, 0, step_e(1, r, 0, e0, get(H, r, 0), (h[0] + d2, h[1] + d3)))
         put3(lo_h, r, (zero, d2, d3))
-        c = 0.25 * c_lo[...]
+        c = 0.25 * dealt(c_lo)
         put3(lo_e, r, tuple(c * v for v in curl_h((zero, d2, d3), None)))
         e7 = e_at(0, r, 7)
         h7 = next_h(None, e7, pair(recv_e, 0, r))
         put(H, h7, r, 7)
         put_e(1, r, 7, step_e(1, r, 7, e7, h7, (H[r, 1, 6], H[r, 2, 6])))
-        c = m_hi * 0.25 * c_hi[...]
+        c = m_hi * 0.25 * dealt(c_hi)
         put3(hi_e, r, (zero, c * h7[2], -c * h7[1]))
 
     runs(step2)
@@ -294,7 +307,7 @@
         put3(lo_h, r, dh)
         h = pair(recv_h, 1, r)
         put_e(2, r, 0, step_e(2, r, 0, e0, get(H, r, 0), (h[0] + dh[1], h[1] + dh[2])))
-        c = 0.25 * c_lo[...]
+        c = 0.25 * dealt(c_lo)
         curl = curl_h(dh, (de[2], -de[1]))
         put3(lo_e, r, tuple(de[k] + c * curl[k] for k in range(3)))
         do_e(2, r, 1)
@@ -305,7 +318,7 @@
         put(H, h7, r, 7)
         do_e(2, r, 7)
         do_e(2, r, 6)
-        c = 0.25 * c_hi[...]
+        c = 0.25 * dealt(c_hi)
         curl = curl_h(next_h(None, de, None), (m_hi * h7[1], m_hi * h7[2]))
         put3(hi_e, r, tuple(de[k] + c * curl[k] for k in range(3)))
 
@@ -349,7 +362,7 @@
         for copy in g_copies[piece]:
             copy.wait_recv()
         for p in range(start, start + size):
-            block = G[src, p]
+            block = G[p, share(src), :]
             for d in range(1, nsrc):
                 block = block + R[d - 1, p]
             head = block.astype(jnp.bfloat16)
@@ -388,28 +401,28 @@
         cx, ny, nz = eps.shape
         ys = foot.shape[1]
         f32 = jnp.float32
-        plane = (ny, nz)
+        raw, plane = (ny, nz), (ny // 8, 8, nz)
 
         def vmem(*shape):
             return pltpu.VMEM(shape, f32)
 
         dma = pltpu.SemaphoreType.DMA
-        any_spec = pl.BlockSpec(memory_space=pl.ANY)
+        hbm = pl.BlockSpec(memory_space=pltpu.HBM)
         return pl.pallas_call(
             functools.partial(kernel, n, nsrc),
             out_shape=jax.ShapeDtypeStruct((PIX_DEV, nz), f32),
-            in_specs=[any_spec, any_spec, any_spec, pl.BlockSpec(memory_space=pltpu.SMEM),
-                      pl.BlockSpec(memory_space=pltpu.VMEM)],
+            in_specs=[hbm, hbm, hbm, pl.BlockSpec(memory_space=pltpu.SMEM), hbm],
             out_specs=pl.BlockSpec(memory_space=pltpu.VMEM),
             scratch_shapes=[
+                pltpu.VMEM(foot.shape, jnp.int32), vmem(2, 3, cx, *raw), vmem(cx, *raw),
                 vmem(2, 3, cx, *plane), vmem(cx, *plane), vmem(ITERS, 2, 3, cx, *plane),
                 vmem(2, 3, cx, *plane), vmem(2, 3, *plane), vmem(2, 3, *plane), vmem(2, 3, *plane),
                 vmem(3, 2, 2, *plane), vmem(3, 2, 2, *plane), vmem(3, 2, 2, *plane), vmem(3, 2, 2, *plane),
-                vmem(*plane), vmem(*plane),
+                vmem(*raw), vmem(*raw),
                 vmem(2, 3, *plane), vmem(2, 3, *plane), vmem(2, 3, *plane), vmem(2, 8, 128),
-                vmem(nsrc, cx, ys, nz), vmem(nsrc - 1, cx, ys, nz),
+                vmem(cx, *raw), vmem(nsrc - 1, cx, ys, nz),
                 vmem(n, PIX_DEV, nz), vmem(n - 1, PIX_DEV, nz),
-                dma((3,)), dma((4,)), dma((4,)), dma((4,)), dma((4,)),
+                dma((4,)), dma((4,)), dma((4,)), dma((4,)), dma((4,)),
                 dma((nsrc - 1, 3)), dma((nsrc - 1, 3)), dma((n - 1,)), dma((n - 1,)),
             ],
             compiler_params=pltpu.CompilerParams(

time: 31.2 us -> 31.2 us (level)
  no operation moved by 1% of the time
where the time goes in v2:
time: 31.2 us; the launch traced here: 31 us
  Pallas kernels  25.8 us (83%)
  local copies, waits for them, and re-layouts  4.5 us (14%)
  between operations  0.67 us (2%)
    pallas_call x1, Pallas kernels, per_device(): pl.pallas_call(functools.partial(kernel, n, nsrc), out_shape=jax.ShapeDty...  25.8 us
    unnamed x9, local copies, waits for them, and re-layouts  4.5 us

profile of v2, /device:TPU:0, one launch (start us, length us, event | category | flops | bytes accessed | tf_op | source)
XLA Modules:
  0.0 31.0 jit_solution(5460486269374519902)
XLA Ops:
  0.7 0.0 copy-start
  0.7 1.1 %copy-done = f32[1,3,8,64,128]{4,3,2,1,0:T(8,128)S(1)} copy-done((f32[1,3,8,64,128]{4,3,2,1,0:T(8,128)S(1)}, f32[1,3,8,64,128]{4,3,2,1,0:T(8,128)}, u32[]{:S(2)}) %copy-start) | copy-done | bytes 786456
  1.8 0.0 copy-start.1
  1.8 1.1 %copy-done.1 = f32[1,3,8,64,128]{4,3,2,1,0:T(8,128)S(1)} copy-done((f32[1,3,8,64,128]{4,3,2,1,0:T(8,128)S(1)}, f32[1,3,8,64,128]{4,3,2,1,0:T(8,128)}, u32[]{:S(2)}) %copy-start.1) | copy-done | bytes 786456
  2.9 0.0 copy-start.2
  2.9 0.9 %copy-done.2 = f32[8,64,128]{2,1,0:T(8,128)S(1)} copy-done((f32[8,64,128]{2,1,0:T(8,128)S(1)}, f32[8,64,128]{2,1,0:T(8,128)}, u32[]{:S(2)}) %copy-start.2) | copy-done | bytes 262168
  3.9 0.0 copy-start.3
  3.9 0.7 %copy-done.3 = s32[8,32]{1,0:T(8,128)S(1)} copy-done((s32[8,32]{1,0:T(8,128)S(1)}, s32[8,32]{1,0:T(8,128)}, u32[]{:S(2)}) %copy-start.3) | copy-done | bytes 1048
  4.6 25.8 %shard_map.55 = f32[16,128]{1,0:T(8,128)S(1)} custom-call(f32[1,3,8,64,128]{4,3,2,1,0:T(8,128)S(1)} %copy-done, f32[1,3,8,64,128]{4,3,2,1,0:T(8,128)S(1)} %copy-done.1, f32[8,64,128]{2,1,0:T(8,128)S(1)} %copy-done.2, s32[1]{0:T(128)S(6)} %copy.7.wave, s32[8,32]{1,0:T(8,128)S(1)} %copy-done.3), custom_call_target="tpu_custom_call" | custom-call | flops 30000000 | bytes 2000000 | tf_op jit(solution)/shard_map/pallas_call | solution.py:411
  30.4 0.6 %copy.8 = f32[16,128]{1,0:T(8,128)} copy(f32[16,128]{1,0:T(8,128)S(1)} %shard_map.55) | data formatting | bytes 16384
Async XLA Ops:
  0.7 1.1 %copy-start = (f32[1,3,8,64,128]{4,3,2,1,0:T(8,128)S(1)}, f32[1,3,8,64,128]{4,3,2,1,0:T(8,128)}, u32[]{:S(2)}) copy-start(f32[1,3,8,64,128]{4,3,2,1,0:T(8,128)} %fwd.1) | copy-start | bytes 2359300
  1.8 1.1 %copy-start.1 = (f32[1,3,8,64,128]{4,3,2,1,0:T(8,128)S(1)}, f32[1,3,8,64,128]{4,3,2,1,0:T(8,128)}, u32[]{:S(2)}) copy-start(f32[1,3,8,64,128]{4,3,2,1,0:T(8,128)} %adj.1) | copy-start | bytes 2359300
  2.9 0.9 %copy-start.2 = (f32[8,64,128]{2,1,0:T(8,128)S(1)}, f32[8,64,128]{2,1,0:T(8,128)}, u32[]{:S(2)}) copy-start(f32[8,64,128]{2,1,0:T(8,128)} %eps.1) | copy-start | bytes 786436
  3.9 0.7 %copy-start.3 = (s32[8,32]{1,0:T(8,128)S(1)}, s32[8,32]{1,0:T(8,128)}, u32[]{:S(2)}) copy-start(s32[8,32]{1,0:T(8,128)} %foot_hbm.1) | copy-start | bytes 3076

commit v3 on v2

--- a/solution.py
+++ b/solution.py
@@ -9,7 +9,7 @@
 
 ITERS = 4
 PIX_DEV = 16
-PIECES = ((3, 2), (0, 3), (5, 3))
+PIECES = ((2, 4), (1, 1), (6, 1), (0, 1), (7, 1))
 MESH = pl.DeviceIdType.MESH
 
 
@@ -56,8 +56,8 @@
 
 
 def kernel(n, nsrc, fwd, adj, eps, wave, foot_hbm, out,
-           foot, JR, CR, J, C, E, H, HI, EL, EH, send_e, send_h, recv_e, recv_h, c_lo, c_hi,
-           lo_h, lo_e, hi_e, sig, G, R, T, RT,
+           foot, JR, CR, J, C, E, H, HI, EL, EH, send_e, send_h, recv_e, recv_h, c_lo, c_hi, j_lo, j_hi,
+           q_lo, q_hi, r_lo, r_hi, b_lo, b_hi, e_lo, e_hi, lo_h, lo_e, hi_e, sig, G, R, T, RT,
            load_sem, es_sem, er_sem, hs_sem, hr_sem, gs_sem, gr_sem, ts_sem, tr_sem):
     me = lax.axis_index("space")
     src = lax.axis_index("src")
@@ -89,30 +89,35 @@
         return pltpu.make_async_remote_copy(
             src_ref=a, dst_ref=b, send_sem=s, recv_sem=r, device_id=where, device_id_type=MESH)
 
-    e_copies = [remote(send_e.at[t], recv_e.at[t], es_sem.at[t], er_sem.at[t], {"space": low}) for t in range(3)]
-    e_copies.append(remote(eps.at[0], c_hi, es_sem.at[3], er_sem.at[3], {"space": low}))
-    h_copies = [remote(send_h.at[t], recv_h.at[t], hs_sem.at[t], hr_sem.at[t], {"space": high}) for t in range(3)]
-    h_copies.append(remote(eps.at[7], c_lo, hs_sem.at[3], hr_sem.at[3], {"space": high}))
-
-    def start_e(t):
-        pl.when(has_low)(lambda: e_copies[t].start())
-
-    def start_h(t):
-        pl.when(has_high)(lambda: h_copies[t].start())
-
-    def arrived(t):
-        pl.when(has_low)(lambda: h_copies[t].wait_recv())
-        pl.when(has_high)(lambda: e_copies[t].wait_recv())
+    def copies(pairs, s, r, where):
+        return [remote(a, b, s.at[i], r.at[i], where) for i, (a, b) in enumerate(pairs)]
+
+    e_copies = copies((
+        (fwd.at[0, pl.ds(1, 2), 0], j_hi.at[0]), (adj.at[0, pl.ds(1, 2), 0], j_hi.at[1]), (eps.at[0], c_hi),
+        (send_e, recv_e), (q_lo, r_hi)), es_sem, er_sem, {"space": low})
+    h_copies = copies((
+        (fwd.at[0, :, 7], j_lo.at[0]), (adj.at[0, :, 7], j_lo.at[1]), (eps.at[7], c_lo),
+        (send_h, recv_h), (q_hi, r_lo)), hs_sem, hr_sem, {"space": high})
+
+    def start_e(*those):
+        pl.when(has_low)(lambda: [e_copies[i].start() for i in those] and None)
+
+    def start_h(*those):
+        pl.when(has_high)(lambda: [h_copies[i].start() for i in those] and None)
+
+    def arrived(*those):
+        pl.when(has_low)(lambda: [h_copies[i].wait_recv() for i in those] and None)
+        pl.when(has_high)(lambda: [e_copies[i].wait_recv() for i in those] and None)
 
     @pl.when(jnp.logical_not(has_low))
     def _():
-        recv_h[...] = jnp.zeros_like(recv_h)
-        c_lo[...] = jnp.zeros_like(c_lo)
+        for ref in (recv_h, c_lo, j_lo, r_lo):
+            ref[...] = jnp.zeros_like(ref)
 
     @pl.when(jnp.logical_not(has_high))
     def _():
-        recv_e[...] = jnp.zeros_like(recv_e)
-        c_hi[...] = jnp.zeros_like(c_hi)
+        for ref in (recv_e, c_hi, j_hi, r_hi):
+            ref[...] = jnp.zeros_like(ref)
 
     m_lo = jnp.where(has_low, 1.0, 0.0).astype(jnp.float32)
     m_hi = jnp.where(has_high, 1.0, 0.0).astype(jnp.float32)
@@ -131,11 +136,11 @@
         for k in range(3):
             ref[r, k] = vals[k]
 
-    def pair(ref, t, r):
-        return ref[t, r, 0], ref[t, r, 1]
-
-    def put_pair(ref, t, r, vals):
-        ref[t, r, 0], ref[t, r, 1] = vals[1], vals[2]
+    def pair(ref, r):
+        return ref[r, 0], ref[r, 1]
+
+    def put_pair(ref, r, vals):
+        ref[r, 0], ref[r, 1] = vals[1], vals[2]
 
     def e_at(t, r, p):
         return tuple(E[t, r, k, p] for k in range(3))
@@ -176,6 +181,9 @@
             J[r, k, p] = a
             E[0, r, k, p] = -s * a
 
+    pl.semaphore_wait(barrier, n - 1 + nsrc - 1)
+    start_e(0, 1, 2)
+    start_h(0, 1, 2)
     for copy in loads:
         copy.wait()
 
@@ -184,61 +192,40 @@
         return 0
 
     lax.fori_loop(0, 8, scale, 0)
-
-    def first(r):
-        begin(r, 0)
-        put_pair(send_e, 0, r, e_at(0, r, 0))
-        begin(r, 7)
-        h = next_h(None, e_at(0, r, 7), None)
-        put3(HI, r, h)
-        put_pair(send_h, 0, r, h)
-
-    runs(first)
-    pl.semaphore_wait(barrier, n - 1 + nsrc - 1)
-    start_e(3)
-    start_h(3)
-    start_e(0)
-    start_h(0)
-    planes(1, 7, begin)
+    planes(0, 8, begin)
     planes(0, 7, functools.partial(do_h, 0))
 
-    def second(r):
+    def alone_low(r):
         e = step_e(1, r, 0, e_at(0, r, 0), get(H, r, 0), None)
         put3(EL, r, e)
-        put_pair(send_e, 1, r, e)
-
-    runs(second)
-    start_e(1)
-
-    def third(r):
+        put_pair(send_e, r, e)
+
+    runs(alone_low)
+    start_e(3)
+
+    def alone_high(r):
         do_e(1, r, 6)
-        h7 = get3(HI, r)
+        h7 = next_h(None, e_at(0, r, 7), None)
         e7 = step_e(1, r, 7, e_at(0, r, 7), h7, (H[r, 1, 6], H[r, 2, 6]))
         put3(EH, r, e7)
         h7 = next_h(h7, e7, None)
         put3(HI, r, h7)
-        put_pair(send_h, 1, r, h7)
-
-    runs(third)
-    start_h(1)
-
-    def fourth(r):
+        put_pair(send_h, r, h7)
+
+    runs(alone_high)
+    start_h(3)
+
+    def alone_last(r):
         do_e(1, r, 1)
         e = get3(EL, r)
         h = next_h(get(H, r, 0), e, (E[1, r, 1, 1], E[1, r, 2, 1]))
-        put_pair(send_e, 2, r, step_e(2, r, 0, e, h, None))
-
-    runs(fourth)
-    start_e(2)
-
-    def fifth(r):
+        put3(EL, r, step_e(2, r, 0, e, h, None))
         e7, h7 = get3(EH, r), get3(HI, r)
         h6 = next_h(get(H, r, 6), e_at(1, r, 6), (e7[1], e7[2]))
         e7 = step_e(2, r, 7, e7, h7, (h6[1], h6[2]))
-        put_pair(send_h, 2, r, next_h(h7, e7, None))
-
-    runs(fifth)
-    start_h(2)
+        put3(HI, r, next_h(h7, e7, None))
+
+    runs(alone_last)
 
     planes(2, 6, functools.partial(do_e, 1))
     planes(1, 6, functools.partial(do_h, 1))
@@ -246,8 +233,33 @@
     planes(2, 5, functools.partial(do_h, 2))
     planes(3, 5, functools.partial(do_e, 3))
 
-    def product(p):
-        total = None
+    arrived(0, 1, 2)
+    b_lo[...] = 0.25 * dealt(c_lo)
+    b_hi[...] = 0.25 * dealt(c_hi)
+
+    def edges(r):
+        s = sig[r, 0:1, :]
+        for k in range(3):
+            e_lo[r, k] = -s * (2.0 * b_lo[...] * dealt(j_lo, r, k))
+        for k in range(2):
+            e_hi[r, k] = -s * (2.0 * b_hi[...] * dealt(j_hi, r, k))
+
+    runs(edges)
+    for_low, for_high = None, None
+    for r in range(2):
+        curl = curl_h((jnp.zeros_like(EL[r, 0]), EL[r, 2], -EL[r, 1]), None)
+        terms = [e_lo[1 - r, k] * curl[k] for k in range(3)]
+        term = terms[0] + terms[1] + terms[2]
+        for_low = term if for_low is None else for_low + term
+        term = e_hi[1 - r, 0] * HI[r, 2] - e_hi[1 - r, 1] * HI[r, 1]
+        for_high = term if for_high is None else for_high + term
+    q_lo[...] = b_lo[...] * for_low
+    q_hi[...] = b_hi[...] * for_high
+    start_e(4)
+    start_h(4)
+
+    def product(p, more=None):
+        total = more
         for t in range(ITERS):
             for k in range(3):
                 term = E[t, 0, k, p] * E[ITERS - 1 - t, 1, k, p]
@@ -256,9 +268,6 @@
         for j in range(folds):
             G[p, pl.ds(j, 8, stride=folds), :] = total[j]
 
-    def products(a, b):
-        lax.fori_loop(a, b, lambda p, _: (product(p), 0)[1], 0)
-
     def share(j):
         return pl.ds(pl.multiple_of(j * ys, 8), ys)
 
@@ -274,101 +283,97 @@
         for copy in g_copies[piece]:
             copy.start()
 
-    products(3, 5)
-    start_g(0)
-
-    arrived(3)
-    arrived(0)
-
     def step2(r):
         e0 = e_at(0, r, 0)
         d2, d3 = m_lo * e0[2], -m_lo * e0[1]
         zero = jnp.zeros_like(d2)
-        h = pair(recv_h, 0, r)
-        put_e(1, r, 0, step_e(1, r, 0, e0, get(H, r, 0), (h[0] + d2, h[1] + d3)))
+        h = next_h(None, get3(e_lo, r), None)
+        put_e(1, r, 0, step_e(1, r, 0, e0, get(H, r, 0), (h[1] + d2, h[2] + d3)))
         put3(lo_h, r, (zero, d2, d3))
-        c = 0.25 * dealt(c_lo)
-        put3(lo_e, r, tuple(c * v for v in curl_h((zero, d2, d3), None)))
+        put3(lo_e, r, tuple(b_lo[...] * v for v in curl_h((zero, d2, d3), None)))
         e7 = e_at(0, r, 7)
-        h7 = next_h(None, e7, pair(recv_e, 0, r))
+        h7 = next_h(None, e7, pair(e_hi, r))
         put(H, h7, r, 7)
         put_e(1, r, 7, step_e(1, r, 7, e7, h7, (H[r, 1, 6], H[r, 2, 6])))
-        c = m_hi * 0.25 * dealt(c_hi)
+        c = m_hi * b_hi[...]
         put3(hi_e, r, (zero, c * h7[2], -c * h7[1]))
+        do_h(1, r, 0)
+        do_e(2, r, 1)
+        do_h(2, r, 1)
+        do_e(3, r, 2)
+        do_h(1, r, 6)
+        do_e(2, r, 6)
+        do_h(2, r, 5)
+        do_e(3, r, 5)
 
     runs(step2)
-    arrived(1)
-
-    def step3(r):
-        do_h(1, r, 0)
+    lax.fori_loop(2, 6, lambda p, _: (product(p), 0)[1], 0)
+    start_g(0)
+    arrived(3)
+
+    def step3_low(r):
         e0 = e_at(1, r, 0)
         de = get3(lo_e, r)
         dh = next_h(get3(lo_h, r), de, (m_lo * e0[1], m_lo * e0[2]))
-        put3(lo_h, r, dh)
-        h = pair(recv_h, 1, r)
-        put_e(2, r, 0, step_e(2, r, 0, e0, get(H, r, 0), (h[0] + dh[1], h[1] + dh[2])))
-        c = 0.25 * dealt(c_lo)
+        h = pair(recv_h, r)
+        new = step_e(2, r, 0, e0, get(H, r, 0), (h[0] + dh[1], h[1] + dh[2]))
+        put_e(2, r, 0, new)
         curl = curl_h(dh, (de[2], -de[1]))
-        put3(lo_e, r, tuple(de[k] + c * curl[k] for k in range(3)))
-        do_e(2, r, 1)
-        do_h(1, r, 6)
+        de = tuple(de[k] + b_lo[...] * curl[k] for k in range(3))
+        dh = next_h(dh, de, (m_lo * new[1], m_lo * new[2]))
+        do_h(2, r, 0)
+        put_e(3, r, 0, step_e(3, r, 0, new, get(H, r, 0), (dh[1], dh[2])))
+        do_e(3, r, 1)
+
+    runs(step3_low)
+    product(1)
+    start_g(1)
+
+    def step3_high(r):
         de = get3(hi_e, r)
-        e = pair(recv_e, 1, r)
+        e = pair(recv_e, r)
         h7 = next_h(get(H, r, 7), e_at(1, r, 7), (e[0] + de[1], e[1] + de[2]))
         put(H, h7, r, 7)
         do_e(2, r, 7)
-        do_e(2, r, 6)
-        c = 0.25 * dealt(c_hi)
         curl = curl_h(next_h(None, de, None), (m_hi * h7[1], m_hi * h7[2]))
-        put3(hi_e, r, tuple(de[k] + c * curl[k] for k in range(3)))
-
-    runs(step3)
-    arrived(2)
-
-    def low4(r):
-        e0 = e_at(2, r, 0)
-        dh = next_h(get3(lo_h, r), get3(lo_e, r), (m_lo * e0[1], m_lo * e0[2]))
-        h = pair(recv_h, 2, r)
-        do_h(2, r, 0)
-        do_h(2, r, 1)
-        put_e(3, r, 0, step_e(3, r, 0, e0, get(H, r, 0), (h[0] + dh[1], h[1] + dh[2])))
-        do_e(3, r, 1)
-        do_e(3, r, 2)
-
-    runs(low4)
-    products(0, 3)
-    start_g(1)
-
-    def high4(r):
-        de = get3(hi_e, r)
-        e = pair(recv_e, 2, r)
-        put(H, next_h(get(H, r, 7), e_at(2, r, 7), (e[0] + de[1], e[1] + de[2])), r, 7)
+        de = tuple(de[k] + b_hi[...] * curl[k] for k in range(3))
+        put(H, next_h(h7, e_at(2, r, 7), (de[1], de[2])), r, 7)
         do_h(2, r, 6)
-        do_h(2, r, 5)
         do_e(3, r, 7)
         do_e(3, r, 6)
-        do_e(3, r, 5)
-
-    runs(high4)
-    products(5, 8)
+
+    runs(step3_high)
+    product(6)
     start_g(2)
+    arrived(4)
+    product(0, r_lo[...])
+    start_g(3)
+    product(7, r_hi[...])
+    start_g(4)
 
     pixels = n * PIX_DEV
     ids = foot[...] - src * pixels
-    row = lax.broadcasted_iota(jnp.int32, (pixels, ys), 0)
-    chosen = [(row == ids[p:p + 1, :]).astype(jnp.float32).astype(jnp.bfloat16) for p in range(8)]
-    total = jnp.zeros((pixels, 128), jnp.float32)
-    for piece, (start, size) in enumerate(PIECES):
-        for copy in g_copies[piece]:
-            copy.wait_recv()
-        for p in range(start, start + size):
-            block = G[p, share(src), :]
-            for d in range(1, nsrc):
-                block = block + R[d - 1, p]
-            head = block.astype(jnp.bfloat16)
-            tail = (block - head.astype(jnp.float32)).astype(jnp.bfloat16)
-            total = total + jnp.dot(chosen[p], head, preferred_element_type=jnp.float32)
-            total = total + jnp.dot(chosen[p], tail, preferred_element_type=jnp.float32)
+    total = None
+    for pieces in ((0,), (1, 2), (3, 4)):
+        heads, tails, chosen = [], [], []
+        for piece in pieces:
+            for copy in g_copies[piece]:
+                copy.wait_recv()
+            start, size = PIECES[piece]
+            for p in range(start, start + size):
+                block = G[p, share(src), :]
+                for d in range(1, nsrc):
+                    block = block + R[d - 1, p]
+                head = block.astype(jnp.bfloat16).astype(jnp.float32)
+                heads.append(head)
+                tails.append(block - head)
+                chosen.append(ids[p:p + 1, :])
+        row = lax.broadcasted_iota(jnp.int32, (pixels, len(chosen) * ys), 0)
+        select = (row == jnp.concatenate(chosen, axis=1)).astype(jnp.float32).astype(jnp.bfloat16)
+        for part in (heads, tails):
+            part = jnp.concatenate(part, axis=0).astype(jnp.bfloat16)
+            term = jnp.dot(select, part, preferred_element_type=jnp.float32)
+            total = term if total is None else total + term
     T[...] = total.reshape(n, PIX_DEV, 128)
 
     t_copies = [
@@ -389,9 +394,8 @@
     for piece in g_copies:
         for copy in piece:
             copy.wait_send()
-    for t in range(4):
-        pl.when(has_low)(lambda: e_copies[t].wait_send())
-        pl.when(has_high)(lambda: h_copies[t].wait_send())
+    pl.when(has_low)(lambda: [copy.wait_send() for copy in e_copies] and None)
+    pl.when(has_high)(lambda: [copy.wait_send() for copy in h_copies] and None)
 
 
 def solution(mesh):
@@ -417,16 +421,18 @@
                 pltpu.VMEM(foot.shape, jnp.int32), vmem(2, 3, cx, *raw), vmem(cx, *raw),
                 vmem(2, 3, cx, *plane), vmem(cx, *plane), vmem(ITERS, 2, 3, cx, *plane),
                 vmem(2, 3, cx, *plane), vmem(2, 3, *plane), vmem(2, 3, *plane), vmem(2, 3, *plane),
-                vmem(3, 2, 2, *plane), vmem(3, 2, 2, *plane), vmem(3, 2, 2, *plane), vmem(3, 2, 2, *plane),
-                vmem(*raw), vmem(*raw),
+                vmem(2, 2, *plane), vmem(2, 2, *plane), vmem(2, 2, *plane), vmem(2, 2, *plane),
+                vmem(*raw), vmem(*raw), vmem(2, 3, *raw), vmem(2, 2, *raw),
+                vmem(*plane), vmem(*plane), vmem(*plane), vmem(*plane), vmem(*plane), vmem(*plane),
+                vmem(2, 3, *plane), vmem(2, 2, *plane),
                 vmem(2, 3, *plane), vmem(2, 3, *plane), vmem(2, 3, *plane), vmem(2, 8, 128),
                 vmem(cx, *raw), vmem(nsrc - 1, cx, ys, nz),
                 vmem(n, PIX_DEV, nz), vmem(n - 1, PIX_DEV, nz),
-                dma((4,)), dma((4,)), dma((4,)), dma((4,)), dma((4,)),
-                dma((nsrc - 1, 3)), dma((nsrc - 1, 3)), dma((n - 1,)), dma((n - 1,)),
+                dma((4,)), dma((5,)), dma((5,)), dma((5,)), dma((5,)),
+                dma((nsrc - 1, len(PIECES))), dma((nsrc - 1, len(PIECES))), dma((n - 1,)), dma((n - 1,)),
             ],
             compiler_params=pltpu.CompilerParams(
-                collective_id=0, has_side_effects=True, vmem_limit_bytes=40 * 1024 * 1024),
+                collective_id=0, has_side_effects=True, vmem_limit_bytes=60 * 1024 * 1024),
             cost_estimate=pl.CostEstimate(flops=30_000_000, bytes_accessed=2_000_000, transcendentals=0),
         )(fwd, adj, eps, wave, foot)
 

time: 31.2 us -> 27.2 us (0.87)
  local copies, waits for them, and re-layouts: 4.5 us -> 1.3 us
  Pallas kernels: 25.8 us -> 25 us
    unnamed x9 -> x1, local copies, waits for them, and re-layouts: 4.5 us -> 1.3 us
    pallas_call x1, Pallas kernels: 25.8 us -> 25 us  [per_device(): pl.pallas_call(functools.partial(kernel, n, nsrc), out_shape=jax.ShapeDty...]
where the time goes in v3:
time: 27.2 us; the launch traced here: 27 us
  Pallas kernels  25 us (92%)
  local copies, waits for them, and re-layouts  1.3 us (5%)
  between operations  0.66 us (2%)
    pallas_call x1, Pallas kernels, per_device(): pl.pallas_call(functools.partial(kernel, n, nsrc), out_shape=jax.ShapeDty...  25 us
    unnamed x1, local copies, waits for them, and re-layouts  1.3 us

profile of v3, /device:TPU:0, one launch (start us, length us, event | category | flops | bytes accessed | tf_op | source)
XLA Modules:
  0.0 27.0 jit_solution(5717583239169726730)
XLA Ops:
  0.7 25.0 %shard_map.55 = f32[16,128]{1,0:T(8,128)} custom-call(f32[1,3,8,64,128]{4,3,2,1,0:T(8,128)} %fwd.1, f32[1,3,8,64,128]{4,3,2,1,0:T(8,128)} %adj.1, f32[8,64,128]{2,1,0:T(8,128)} %eps.1, s32[1]{0:T(128)S(6)} %copy.7.wave, s32[8,32]{1,0:T(8,128)} %foot_hbm.1), custom_call_target="tpu_custom_call" | custom-call | flops 30000000 | bytes 2000000 | tf_op jit(solution)/shard_map/pallas_call | solution.py:415
  25.7 1.3 %copy.8 = f32[16,128]{1,0:T(8,128)} copy(f32[16,128]{1,0:T(8,128)} %shard_map.55) | data formatting | bytes 16384

commit v4 on v3

--- a/solution.py
+++ b/solution.py
@@ -57,10 +57,12 @@
 
 def kernel(n, nsrc, fwd, adj, eps, wave, foot_hbm, out,
            foot, JR, CR, J, C, E, H, HI, EL, EH, send_e, send_h, recv_e, recv_h, c_lo, c_hi, j_lo, j_hi,
-           q_lo, q_hi, r_lo, r_hi, b_lo, b_hi, e_lo, e_hi, lo_h, lo_e, hi_e, sig, G, R, T, RT,
-           load_sem, es_sem, er_sem, hs_sem, hr_sem, gs_sem, gr_sem, ts_sem, tr_sem):
+           q_lo, q_hi, r_lo, r_hi, b_lo, b_hi, e_lo, e_hi, lo_h, lo_e, hi_e, sig, G, R, T, S, U, RT,
+           load_sem, es_sem, er_sem, hs_sem, hr_sem, gs_sem, gr_sem, ss_sem, ts_sem, tr_sem):
     me = lax.axis_index("space")
     src = lax.axis_index("src")
+    chips, chip, core = n // 2, me // 2, lax.rem(me, 2)
+    sibling = 2 * chip + 1 - core
     low, high = lax.rem(me + n - 1, n), lax.rem(me + 1, n)
     has_low, has_high = me > 0, me < n - 1
     ys = foot.shape[1]
@@ -75,8 +77,9 @@
         copy.start()
 
     barrier = pltpu.get_barrier_semaphore()
-    for d in range(1, n):
-        pl.semaphore_signal(barrier, inc=1, device_id={"space": lax.rem(me + d, n)}, device_id_type=MESH)
+    partners = [sibling, lax.rem(me + n + 2 * core - 1, n)] + [2 * lax.rem(chip + d, chips) + core for d in range(1, chips)]
+    for device in partners:
+        pl.semaphore_signal(barrier, inc=1, device_id={"space": device}, device_id_type=MESH)
     for d in range(1, nsrc):
         pl.semaphore_signal(barrier, inc=1, device_id={"src": lax.rem(src + d, nsrc)}, device_id_type=MESH)
 
@@ -181,7 +184,7 @@
             J[r, k, p] = a
             E[0, r, k, p] = -s * a
 
-    pl.semaphore_wait(barrier, n - 1 + nsrc - 1)
+    pl.semaphore_wait(barrier, chips + 1 + nsrc - 1)
     start_e(0, 1, 2)
     start_h(0, 1, 2)
     for copy in loads:
@@ -374,21 +377,27 @@
             part = jnp.concatenate(part, axis=0).astype(jnp.bfloat16)
             term = jnp.dot(select, part, preferred_element_type=jnp.float32)
             total = term if total is None else total + term
-    T[...] = total.reshape(n, PIX_DEV, 128)
+    for owner in range(n):
+        T[owner % 2, owner // 2] = total[owner * PIX_DEV:(owner + 1) * PIX_DEV]
+    swap = remote(T.at[1 - core], S, ss_sem.at[0], ss_sem.at[1], {"space": sibling})
+    swap.start()
+    swap.wait_recv()
+    U[...] = T[core] + S[...]
 
     t_copies = [
-        remote(T.at[lax.rem(me + d, n)], RT.at[d - 1], ts_sem.at[d - 1], tr_sem.at[d - 1],
-               {"space": lax.rem(me + d, n)})
-        for d in range(1, n)
+        remote(U.at[lax.rem(chip + d, chips)], RT.at[d - 1], ts_sem.at[d - 1], tr_sem.at[d - 1],
+               {"space": 2 * lax.rem(chip + d, chips) + core})
+        for d in range(1, chips)
     ]
     for copy in t_copies:
         copy.start()
-    result = T[me]
-    for d in range(1, n):
+    result = U[chip]
+    for d in range(1, chips):
         t_copies[d - 1].wait_recv()
         result = result + RT[d - 1]
     out[...] = result
 
+    swap.wait_send()
     for copy in t_copies:
         copy.wait_send()
     for piece in g_copies:
@@ -427,9 +436,10 @@
                 vmem(2, 3, *plane), vmem(2, 2, *plane),
                 vmem(2, 3, *plane), vmem(2, 3, *plane), vmem(2, 3, *plane), vmem(2, 8, 128),
                 vmem(cx, *raw), vmem(nsrc - 1, cx, ys, nz),
-                vmem(n, PIX_DEV, nz), vmem(n - 1, PIX_DEV, nz),
+                vmem(2, n // 2, PIX_DEV, nz), vmem(n // 2, PIX_DEV, nz), vmem(n // 2, PIX_DEV, nz),
+                vmem(n // 2 - 1, PIX_DEV, nz),
                 dma((4,)), dma((5,)), dma((5,)), dma((5,)), dma((5,)),
-                dma((nsrc - 1, len(PIECES))), dma((nsrc - 1, len(PIECES))), dma((n - 1,)), dma((n - 1,)),
+                dma((nsrc - 1, len(PIECES))), dma((nsrc - 1, len(PIECES))), dma((2,)), dma((n // 2 - 1,)), dma((n // 2 - 1,)),
             ],
             compiler_params=pltpu.CompilerParams(
                 collective_id=0, has_side_effects=True, vmem_limit_bytes=60 * 1024 * 1024),

time: 27.2 us -> 26.5 us (0.974)
  Pallas kernels: 25 us -> 24.3 us
    pallas_call x1, Pallas kernels: 25 us -> 24.3 us  [per_device(): pl.pallas_call(functools.partial(kernel, n, nsrc), out_shape=jax.ShapeDty...]
where the time goes in v4:
time: 26.5 us; the launch traced here: 26.3 us
  Pallas kernels  24.3 us (92%)
  local copies, waits for them, and re-layouts  1.3 us (5%)
  between operations  0.66 us (2%)
    pallas_call x1, Pallas kernels, per_device(): pl.pallas_call(functools.partial(kernel, n, nsrc), out_shape=jax.ShapeDty...  24.3 us
    unnamed x1, local copies, waits for them, and re-layouts  1.3 us

profile of v4, /device:TPU:0, one launch (start us, length us, event | category | flops | bytes accessed | tf_op | source)
XLA Modules:
  0.0 26.3 jit_solution(7183403123539130277)
XLA Ops:
  0.7 24.3 %shard_map.55 = f32[16,128]{1,0:T(8,128)} custom-call(f32[1,3,8,64,128]{4,3,2,1,0:T(8,128)} %fwd.1, f32[1,3,8,64,128]{4,3,2,1,0:T(8,128)} %adj.1, f32[8,64,128]{2,1,0:T(8,128)} %eps.1, s32[1]{0:T(128)S(6)} %copy.7.wave, s32[8,32]{1,0:T(8,128)} %foot_hbm.1), custom_call_target="tpu_custom_call" | custom-call | flops 30000000 | bytes 2000000 | tf_op jit(solution)/shard_map/pallas_call | solution.py:424
  25.0 1.3 %copy.8 = f32[16,128]{1,0:T(8,128)} copy(f32[16,128]{1,0:T(8,128)} %shard_map.55) | data formatting | bytes 16384

commit v5 on v4

--- a/solution.py
+++ b/solution.py
@@ -153,14 +153,11 @@
         curl = curl_h(h, h_prev)
         return tuple(e[k] + c * curl[k] - s * J[r, k, p] for k in range(3))
 
-    def do_h(t, r, p):
-        e, nxt = e_at(t, r, p), (E[t, r, 1, p + 1], E[t, r, 2, p + 1])
-        put(H, next_h(None if t == 0 else get(H, r, p), e, nxt), r, p)
-
-    def do_e(t, r, p):
-        new = step_e(t, r, p, e_at(t - 1, r, p), get(H, r, p), (H[r, 1, p - 1], H[r, 2, p - 1]))
-        for k in range(3):
-            E[t, r, k, p] = new[k]
+    def h_at(r, p):
+        return tuple(H[r, k, p] for k in range(3))
+
+    def new_h(t, r, p):
+        return next_h(None if t == 0 else h_at(r, p), e_at(t, r, p), (E[t, r, 1, p + 1], E[t, r, 2, p + 1]))
 
     def put_e(t, r, p, new):
         for k in range(3):
@@ -170,19 +167,31 @@
         lax.fori_loop(0, 2, lambda r, _: (body(r), 0)[1], 0)
 
     def planes(first, last, body):
-        def one(p, _):
-            body(0, p)
-            body(1, p)
-            return 0
-
-        lax.fori_loop(first, last, one, 0)
-
-    def begin(r, p):
-        c2, s = 2.0 * C[p], sig[r, 0:1, :]
-        for k in range(3):
-            a = c2 * dealt(JR, r, k, p)
-            J[r, k, p] = a
-            E[0, r, k, p] = -s * a
+        lax.fori_loop(first, last, lambda p, _: (body(p), 0)[1], 0)
+
+    def sweep(t, first, last):
+        hs = [new_h(t, r, first) for r in range(2)]
+        for r in range(2):
+            put(H, hs[r], r, first)
+
+        def body(p):
+            hs = [new_h(t, r, p) for r in range(2)]
+            es = [step_e(t + 1, r, p, e_at(t, r, p), hs[r], (H[r, 1, p - 1], H[r, 2, p - 1])) for r in range(2)]
+            for r in range(2):
+                put(H, hs[r], r, p)
+                put_e(t + 1, r, p, es[r])
+
+        planes(first + 1, last, body)
+
+    def begin(p):
+        c = 0.25 * dealt(CR, p)
+        for r in range(2):
+            s = sig[r, 0:1, :]
+            for k in range(3):
+                a = 2.0 * c * dealt(JR, r, k, p)
+                J[r, k, p] = a
+                E[0, r, k, p] = -s * a
+        C[p] = c
 
     pl.semaphore_wait(barrier, chips + 1 + nsrc - 1)
     start_e(0, 1, 2)
@@ -190,51 +199,27 @@
     for copy in loads:
         copy.wait()
 
-    def scale(p, _):
-        C[p] = 0.25 * dealt(CR, p)
-        return 0
-
-    lax.fori_loop(0, 8, scale, 0)
     planes(0, 8, begin)
-    planes(0, 7, functools.partial(do_h, 0))
-
-    def alone_low(r):
-        e = step_e(1, r, 0, e_at(0, r, 0), get(H, r, 0), None)
-        put3(EL, r, e)
-        put_pair(send_e, r, e)
-
-    runs(alone_low)
+    sweep(0, 0, 7)
+
+    def alone(r):
+        h0, h6, e1, e2, e3 = h_at(r, 0), h_at(r, 6), e_at(0, r, 0), e_at(1, r, 1), e_at(0, r, 7)
+        e6 = e_at(1, r, 6)
+        h7 = next_h(None, e3, None)
+        e7 = step_e(1, r, 7, e3, h7, h6[1:])
+        h7 = next_h(h7, e7, None)
+        e0 = step_e(1, r, 0, e1, h0, None)
+        put_pair(send_e, r, e0)
+        put_pair(send_h, r, h7)
+        put3(EL, r, step_e(2, r, 0, e0, next_h(h0, e0, e2[1:]), None))
+        h6 = next_h(h6, e6, e7[1:])
+        put3(HI, r, next_h(h7, step_e(2, r, 7, e7, h7, h6[1:]), None))
+
+    runs(alone)
     start_e(3)
-
-    def alone_high(r):
-        do_e(1, r, 6)
-        h7 = next_h(None, e_at(0, r, 7), None)
-        e7 = step_e(1, r, 7, e_at(0, r, 7), h7, (H[r, 1, 6], H[r, 2, 6]))
-        put3(EH, r, e7)
-        h7 = next_h(h7, e7, None)
-        put3(HI, r, h7)
-        put_pair(send_h, r, h7)
-
-    runs(alone_high)
     start_h(3)
-
-    def alone_last(r):
-        do_e(1, r, 1)
-        e = get3(EL, r)
-        h = next_h(get(H, r, 0), e, (E[1, r, 1, 1], E[1, r, 2, 1]))
-        put3(EL, r, step_e(2, r, 0, e, h, None))
-        e7, h7 = get3(EH, r), get3(HI, r)
-        h6 = next_h(get(H, r, 6), e_at(1, r, 6), (e7[1], e7[2]))
-        e7 = step_e(2, r, 7, e7, h7, (h6[1], h6[2]))
-        put3(HI, r, next_h(h7, e7, None))
-
-    runs(alone_last)
-
-    planes(2, 6, functools.partial(do_e, 1))
-    planes(1, 6, functools.partial(do_h, 1))
-    planes(2, 6, functools.partial(do_e, 2))
-    planes(2, 5, functools.partial(do_h, 2))
-    planes(3, 5, functools.partial(do_e, 3))
+    sweep(1, 1, 6)
+    sweep(2, 2, 5)
 
     arrived(0, 1, 2)
     b_lo[...] = 0.25 * dealt(c_lo)
@@ -287,65 +272,65 @@
             copy.start()
 
     def step2(r):
-        e0 = e_at(0, r, 0)
+        e0, e7, h0, h1, h5, h6 = e_at(0, r, 0), e_at(0, r, 7), h_at(r, 0), h_at(r, 1), h_at(r, 5), h_at(r, 6)
+        e1, e6, f2, f5 = e_at(1, r, 1), e_at(1, r, 6), e_at(2, r, 2), e_at(2, r, 5)
         d2, d3 = m_lo * e0[2], -m_lo * e0[1]
         zero = jnp.zeros_like(d2)
         h = next_h(None, get3(e_lo, r), None)
-        put_e(1, r, 0, step_e(1, r, 0, e0, get(H, r, 0), (h[1] + d2, h[2] + d3)))
+        e0 = step_e(1, r, 0, e0, h0, (h[1] + d2, h[2] + d3))
+        de = tuple(b_lo[...] * v for v in curl_h((zero, d2, d3), None))
+        h0 = next_h(h0, e0, e1[1:])
+        f1 = step_e(2, r, 1, e1, h1, h0[1:])
+        h1 = next_h(h1, f1, f2[1:])
+        g2 = step_e(3, r, 2, f2, h_at(r, 2), h1[1:])
+        h7 = next_h(None, e7, pair(e_hi, r))
+        e7 = step_e(1, r, 7, e7, h7, h6[1:])
+        c = m_hi * b_hi[...]
+        h6 = next_h(h6, e6, e7[1:])
+        f6 = step_e(2, r, 6, e6, h6, h5[1:])
+        h5 = next_h(h5, f5, f6[1:])
+        g5 = step_e(3, r, 5, f5, h5, (H[r, 1, 4], H[r, 2, 4]))
         put3(lo_h, r, (zero, d2, d3))
-        put3(lo_e, r, tuple(b_lo[...] * v for v in curl_h((zero, d2, d3), None)))
-        e7 = e_at(0, r, 7)
-        h7 = next_h(None, e7, pair(e_hi, r))
-        put(H, h7, r, 7)
-        put_e(1, r, 7, step_e(1, r, 7, e7, h7, (H[r, 1, 6], H[r, 2, 6])))
-        c = m_hi * b_hi[...]
+        put3(lo_e, r, de)
         put3(hi_e, r, (zero, c * h7[2], -c * h7[1]))
-        do_h(1, r, 0)
-        do_e(2, r, 1)
-        do_h(2, r, 1)
-        do_e(3, r, 2)
-        do_h(1, r, 6)
-        do_e(2, r, 6)
-        do_h(2, r, 5)
-        do_e(3, r, 5)
+        for p, h in ((0, h0), (1, h1), (5, h5), (6, h6), (7, h7)):
+            put(H, h, r, p)
+        for t, p, e in ((1, 0, e0), (2, 1, f1), (3, 2, g2), (1, 7, e7), (2, 6, f6), (3, 5, g5)):
+            put_e(t, r, p, e)
 
     runs(step2)
     lax.fori_loop(2, 6, lambda p, _: (product(p), 0)[1], 0)
     start_g(0)
     arrived(3)
 
-    def step3_low(r):
-        e0 = e_at(1, r, 0)
-        de = get3(lo_e, r)
-        dh = next_h(get3(lo_h, r), de, (m_lo * e0[1], m_lo * e0[2]))
+    def step3(r):
+        e0, e7, f1, f6 = e_at(1, r, 0), e_at(1, r, 7), e_at(2, r, 1), e_at(2, r, 6)
+        h0, h6, h7 = h_at(r, 0), h_at(r, 6), h_at(r, 7)
+        de, dh = get3(lo_e, r), get3(lo_h, r)
+        dh = next_h(dh, de, (m_lo * e0[1], m_lo * e0[2]))
         h = pair(recv_h, r)
-        new = step_e(2, r, 0, e0, get(H, r, 0), (h[0] + dh[1], h[1] + dh[2]))
-        put_e(2, r, 0, new)
+        f0 = step_e(2, r, 0, e0, h0, (h[0] + dh[1], h[1] + dh[2]))
         curl = curl_h(dh, (de[2], -de[1]))
         de = tuple(de[k] + b_lo[...] * curl[k] for k in range(3))
-        dh = next_h(dh, de, (m_lo * new[1], m_lo * new[2]))
-        do_h(2, r, 0)
-        put_e(3, r, 0, step_e(3, r, 0, new, get(H, r, 0), (dh[1], dh[2])))
-        do_e(3, r, 1)
-
-    runs(step3_low)
+        dh = next_h(dh, de, (m_lo * f0[1], m_lo * f0[2]))
+        h0 = next_h(h0, f0, f1[1:])
+        g0 = step_e(3, r, 0, f0, h0, dh[1:])
+        g1 = step_e(3, r, 1, f1, h_at(r, 1), h0[1:])
+        de, e = get3(hi_e, r), pair(recv_e, r)
+        h7 = next_h(h7, e7, (e[0] + de[1], e[1] + de[2]))
+        f7 = step_e(2, r, 7, e7, h7, h6[1:])
+        curl = curl_h(next_h(None, de, None), (m_hi * h7[1], m_hi * h7[2]))
+        de = tuple(de[k] + b_hi[...] * curl[k] for k in range(3))
+        h7 = next_h(h7, f7, de[1:])
+        h6 = next_h(h6, f6, f7[1:])
+        g7 = step_e(3, r, 7, f7, h7, h6[1:])
+        g6 = step_e(3, r, 6, f6, h6, (H[r, 1, 5], H[r, 2, 5]))
+        for t, p, e in ((2, 0, f0), (3, 0, g0), (3, 1, g1), (2, 7, f7), (3, 7, g7), (3, 6, g6)):
+            put_e(t, r, p, e)
+
+    runs(step3)
     product(1)
     start_g(1)
-
-    def step3_high(r):
-        de = get3(hi_e, r)
-        e = pair(recv_e, r)
-        h7 = next_h(get(H, r, 7), e_at(1, r, 7), (e[0] + de[1], e[1] + de[2]))
-        put(H, h7, r, 7)
-        do_e(2, r, 7)
-        curl = curl_h(next_h(None, de, None), (m_hi * h7[1], m_hi * h7[2]))
-        de = tuple(de[k] + b_hi[...] * curl[k] for k in range(3))
-        put(H, next_h(h7, e_at(2, r, 7), (de[1], de[2])), r, 7)
-        do_h(2, r, 6)
-        do_e(3, r, 7)
-        do_e(3, r, 6)
-
-    runs(step3_high)
     product(6)
     start_g(2)
     arrived(4)

time: 26.5 us -> 26.5 us (level)
  no operation moved by 1% of the time
where the time goes in v5:
time: 26.5 us; the launch traced here: 26.3 us
  Pallas kernels  24.3 us (92%)
  local copies, waits for them, and re-layouts  1.3 us (5%)
  between operations  0.66 us (2%)
    pallas_call x1, Pallas kernels, per_device(): pl.pallas_call(functools.partial(kernel, n, nsrc), out_shape=jax.ShapeDty...  24.3 us
    unnamed x1, local copies, waits for them, and re-layouts  1.3 us

profile of v5, /device:TPU:0, one launch (start us, length us, event | category | flops | bytes accessed | tf_op | source)
XLA Modules:
  0.0 26.3 jit_solution(7119096061352880442)
XLA Ops:
  0.7 24.3 %shard_map.55 = f32[16,128]{1,0:T(8,128)} custom-call(f32[1,3,8,64,128]{4,3,2,1,0:T(8,128)} %fwd.1, f32[1,3,8,64,128]{4,3,2,1,0:T(8,128)} %adj.1, f32[8,64,128]{2,1,0:T(8,128)} %eps.1, s32[1]{0:T(128)S(6)} %copy.7.wave, s32[8,32]{1,0:T(8,128)} %foot_hbm.1), custom_call_target="tpu_custom_call" | custom-call | flops 30000000 | bytes 2000000 | tf_op jit(solution)/shard_map/pallas_call | solution.py:409
  25.0 1.3 %copy.8 = f32[16,128]{1,0:T(8,128)} copy(f32[16,128]{1,0:T(8,128)} %shard_map.55) | data formatting | bytes 16384

commit v6 on v5

v6 whole, which is shorter than its diff:
```python
import functools

import jax
import jax.numpy as jnp
from jax import lax
from jax.experimental import pallas as pl
from jax.experimental.pallas import tpu as pltpu
from jax.sharding import PartitionSpec as P

ITERS = 4
PIX_DEV = 16
PIECES = ((3, 2), (1, 2), (5, 2), (0, 1), (7, 1))
MESH = pl.DeviceIdType.MESH


def ahead(f, axis):
    if axis == 1:
        return pltpu.roll(f, f.shape[2] - 1, 2)
    return jnp.concatenate([f[1:], pltpu.roll(f[:1], 7, 1)], axis=0)


def behind(f, axis):
    if axis == 1:
        return pltpu.roll(f, 1, 2)
    return jnp.concatenate([pltpu.roll(f[-1:], 1, 1), f[:-1]], axis=0)


def dealt(ref, *at):
    folds = ref.shape[-2] // 8
    return jnp.stack([ref[(*at, pl.ds(j, 8, stride=folds), slice(None))] for j in range(folds)])


def next_h(h, e, e_next):
    e1, e2, e3 = e
    x2 = -e2 if e_next is None else e_next[0] - e2
    x3 = -e3 if e_next is None else e_next[1] - e3
    curl = (
        (ahead(e3, 0) - e3) - (ahead(e2, 1) - e2),
        (ahead(e1, 1) - e1) - x3,
        x2 - (ahead(e1, 0) - e1),
    )
    if h is None:
        return tuple(-v for v in curl)
    return tuple(a - v for a, v in zip(h, curl))


def curl_h(h, h_prev):
    h1, h2, h3 = h
    x2 = h2 if h_prev is None else h2 - h_prev[0]
    x3 = h3 if h_prev is None else h3 - h_prev[1]
    return (
        (h3 - behind(h3, 0)) - (h2 - behind(h2, 1)),
        (h1 - behind(h1, 1)) - x3,
        x2 - (h1 - behind(h1, 0)),
    )


def kernel(n, nsrc, fwd, adj, eps, wave, foot_hbm, out,
           foot, JR, CR, J, C, E, H, DE, DH, XE, XH, c_lo, c_hi, j_lo, j_hi,
           q_lo, q_hi, RQ, e_lo, sig, G, R, T, S, U, RT,
           load_sem, es_sem, er_sem, hs_sem, hr_sem, gs_sem, gr_sem, ss_sem, ts_sem, tr_sem):
    me = lax.axis_index("space")
    src = lax.axis_index("src")
    chips, chip, core = n // 2, me // 2, lax.rem(me, 2)
    sibling = 2 * chip + 1 - core
    low, high = lax.rem(me + n - 1, n), lax.rem(me + 1, n)
    has_low, has_high = me > 0, me < n - 1
    ys = foot.shape[1]

    loads = [
        pltpu.make_async_copy(eps, CR, load_sem.at[0]),
        pltpu.make_async_copy(fwd.at[0], JR.at[0], load_sem.at[1]),
        pltpu.make_async_copy(adj.at[0], JR.at[1], load_sem.at[2]),
        pltpu.make_async_copy(foot_hbm, foot, load_sem.at[3]),
    ]
    for copy in loads:
        copy.start()

    barrier = pltpu.get_barrier_semaphore()
    partners = [sibling, lax.rem(me + n + 2 * core - 1, n)] + [2 * lax.rem(chip + d, chips) + core for d in range(1, chips)]
    for device in partners:
        pl.semaphore_signal(barrier, inc=1, device_id={"space": device}, device_id_type=MESH)
    for d in range(1, nsrc):
        pl.semaphore_signal(barrier, inc=1, device_id={"src": lax.rem(src + d, nsrc)}, device_id_type=MESH)

    omega = 0.25 + 0.05 * wave[0].astype(jnp.float32)
    when = (lax.broadcasted_iota(jnp.int32, (8, 128), 0) + 1).astype(jnp.float32)
    sig[0] = jnp.sin(omega * when)
    sig[1] = jnp.cos(omega * when)

    def remote(a, b, s, r, where):
        return pltpu.make_async_remote_copy(
            src_ref=a, dst_ref=b, send_sem=s, recv_sem=r, device_id=where, device_id_type=MESH)

    def copies(pairs, s, r, where):
        return [remote(a, b, s.at[i], r.at[i], where) for i, (a, b) in enumerate(pairs)]

    e_copies = copies((
        (fwd.at[0, pl.ds(1, 2), 0], j_hi.at[0]), (adj.at[0, pl.ds(1, 2), 0], j_hi.at[1]), (eps.at[0], c_hi),
        (XE.at[1, 0], XE.at[1, 1]), (q_lo, RQ.at[1])), es_sem, er_sem, {"space": low})
    h_copies = copies((
        (fwd.at[0, :, 7], j_lo.at[0]), (adj.at[0, :, 7], j_lo.at[1]), (eps.at[7], c_lo),
        (XH.at[1, 1], XH.at[1, 0]), (q_hi, RQ.at[0])), hs_sem, hr_sem, {"space": high})

    def start_e(*those):
        pl.when(has_low)(lambda: [e_copies[i].start() for i in those] and None)

    def start_h(*those):
        pl.when(has_high)(lambda: [h_copies[i].start() for i in those] and None)

    def arrived(*those):
        pl.when(has_low)(lambda: [h_copies[i].wait_recv() for i in those] and None)
        pl.when(has_high)(lambda: [e_copies[i].wait_recv() for i in those] and None)

    @pl.when(jnp.logical_not(has_low))
    def _():
        for ref in (XH.at[1, 0], c_lo, j_lo, RQ.at[0]):
            ref[...] = jnp.zeros(ref.shape, jnp.float32)

    @pl.when(jnp.logical_not(has_high))
    def _():
        for ref in (XE.at[1, 1], c_hi, j_hi, RQ.at[1]):
            ref[...] = jnp.zeros(ref.shape, jnp.float32)

    m_lo = jnp.where(has_low, 1.0, 0.0).astype(jnp.float32)
    m_hi = jnp.where(has_high, 1.0, 0.0).astype(jnp.float32)

    def three(ref, *at):
        return tuple(ref[(*at[:-1], k, at[-1])] for k in range(3))

    def put(ref, vals, *at):
        for k in range(3):
            ref[(*at[:-1], k, at[-1])] = vals[k]

    def loop(first, last, body):
        lax.fori_loop(first, last, lambda i, _: (body(i), 0)[1], 0)

    zero = jnp.zeros(C.shape[1:], jnp.float32)

    def begin(p):
        c = 0.25 * dealt(CR, p)
        for r in range(2):
            s = sig[r, 0:1, :]
            for k in range(3):
                a = 2.0 * c * dealt(JR, r, k, p)
                J[r, k, p] = a
                E[0, r, k, p + 1] = -s * a
                H[r, k, p + 1] = zero
        C[p + 3] = c

    def clear(i):
        for r in range(2):
            for k in range(3):
                DE[i // 7, r, k, i % 7] = zero
                DH[i // 7, r, k, i % 7] = zero

    def clear_outside(t):
        for r in range(2):
            for k in range(3):
                E[t, r, k, 9] = zero
                E[t, r, k, 0] = zero
                H[r, k, 0] = zero
            for k in range(2):
                XE[2, 1, r, k] = zero
                XH[2, 0, r, k] = zero

    pl.semaphore_wait(barrier, chips + 1 + nsrc - 1)
    start_e(0, 1, 2)
    start_h(0, 1, 2)
    for copy in loads:
        copy.wait()

    loop(0, 4, clear_outside)
    loop(0, 8, begin)
    for r in range(2):
        for k in range(2):
            XE[0, 0, r, k] = E[0, r, 1 + k, 1]

    def alone(t):
        def body(p):
            es = [three(E, t - 1, r, p + 1) for r in range(2)]
            hs = [next_h(three(H, r, p + 1), es[r], tuple(E[t - 1, r, k, p + 2] for k in (1, 2))) for r in range(2)]
            new = []
            for r in range(2):
                curl, s = curl_h(hs[r], (H[r, 1, p], H[r, 2, p])), sig[r, pl.ds(t, 1), :]
                new.append(tuple(es[r][k] + C[p + 3] * curl[k] - s * J[r, k, p] for k in range(3)))
            for r in range(2):
                put(H, hs[r], r, p + 1)
                put(E, new[r], t, r, p + 1)

        loop(0, 8, body)
        for r in range(2):
            for k in range(2):
                XH[t - 1, 1, r, k] = H[r, 1 + k, 8]

        @pl.when(t < 3)
        def _():
            for r in range(2):
                for k in range(2):
                    XE[t, 0, r, k] = E[t, r, 1 + k, 1]

        @pl.when(t == 2)
        def _():
            start_e(3)
            start_h(3)

    loop(1, ITERS, alone)
    loop(0, 14, clear)

    arrived(0, 1, 2)
    C[2] = 0.25 * dealt(c_lo)
    C[11] = 0.25 * dealt(c_hi)

    def edges(r):
        s = sig[r, 0:1, :]
        low_c, high_c = -2.0 * s * C[2], -2.0 * s * C[11]
        e = tuple(low_c * dealt(j_lo, r, k) for k in range(3))
        h = next_h(None, e, None)
        for k in range(3):
            e_lo[r, k] = e[k]
        for k in range(2):
            XE[0, 1, r, k] = high_c * dealt(j_hi, r, k)
            XH[0, 0, r, k] = h[1 + k]

    loop(0, 2, edges)
    for_low, for_high = None, None
    for r in range(2):
        curl = curl_h((zero, XE[2, 0, r, 1], -XE[2, 0, r, 0]), None)
        terms = [e_lo[1 - r, k] * curl[k] for k in range(3)]
        term = terms[0] + terms[1] + terms[2]
        for_low = term if for_low is None else for_low + term
        term = XE[0, 1, 1 - r, 0] * XH[2, 1, r, 1] - XE[0, 1, 1 - r, 1] * XH[2, 1, r, 0]
        for_high = term if for_high is None else for_high + term
    q_lo[...] = C[2] * for_low
    q_hi[...] = C[11] * for_high
    start_e(4)
    start_h(4)

    def product(p, more=None):
        total = more
        for t in range(ITERS):
            for k in range(3):
                term = E[t, 0, k, p + 1] * E[ITERS - 1 - t, 1, k, p + 1]
                total = term if total is None else total + term
        folds = total.shape[0]
        for j in range(folds):
            G[p, pl.ds(j, 8, stride=folds), :] = total[j]

    def share(j):
        return pl.ds(pl.multiple_of(j * ys, 8), ys)

    g_copies = []
    for piece, (start, size) in enumerate(PIECES):
        g_copies.append([
            remote(G.at[pl.ds(start, size), share(lax.rem(src + d, nsrc))], R.at[d - 1, pl.ds(start, size)],
                   gs_sem.at[d - 1, piece], gr_sem.at[d - 1, piece], {"src": lax.rem(src + d, nsrc)})
            for d in range(1, nsrc)
        ])

    def start_g(piece):
        for copy in g_copies[piece]:
            copy.start()

    loop(3, 5, product)
    start_g(0)

    def correct(t, side):
        is_low = side == 0
        own_e = jnp.where(is_low, m_lo, 1.0)
        own_h = jnp.where(is_low, 1.0, m_hi)

        def magnetic(i):
            m = jnp.where(i == 2, own_e, 0.0)
            hs = []
            for r in range(2):
                nxt = tuple(DE[side, r, 1 + k, i + 1] + m * XE[t - 1, side, r, k] for k in range(2))
                hs.append(next_h(three(DH, side, r, i + 1), three(DE, side, r, i), nxt))
            for r in range(2):
                put(DH, hs[r], side, r, i + 1)

        def electric(i):
            m = jnp.where(i == 3, own_h, 0.0)
            c = C[8 * side + i]
            new = []
            for r in range(2):
                prev = tuple(DH[side, r, 1 + k, i] + m * XH[t - 1, side, r, k] for k in range(2))
                curl = curl_h(three(DH, side, r, i + 1), prev)
                d = three(DE, side, r, i)
                d = tuple(d[k] + c * curl[k] for k in range(3))
                e = three(E, t, r, 8 * side + i - 2)
                new.append((d, tuple(e[k] + d[k] for k in range(3))))
            for r in range(2):
                put(DE, new[r][0], side, r, i)
                put(E, new[r][1], t, r, 8 * side + i - 2)

        last = t == 3
        loop(jnp.where(is_low, jnp.where(t == 2, 1, 2), 3 - t),
             jnp.where(is_low, t + 2, jnp.where(t == 2, 4, 3)), magnetic)
        loop(jnp.where(is_low, jnp.where(last, 3, 2), 3 - t),
             jnp.where(is_low, t + 3, jnp.where(last, 3, 4)), electric)

    def correct_step(t):
        pl.when(t == 2)(lambda: arrived(3))
        loop(0, 2, functools.partial(correct, t))

    loop(1, ITERS, correct_step)
    loop(0, 4, lambda i: product(jnp.where(i < 2, i + 1, i + 3)))
    start_g(1)
    start_g(2)
    arrived(4)
    loop(0, 2, lambda i: product(7 * i, RQ[i]))
    start_g(3)
    start_g(4)

    pixels = n * PIX_DEV
    ids = foot[...] - src * pixels
    total = None
    for pieces in ((0, 1, 2), (3, 4)):
        heads, tails, chosen = [], [], []
        for piece in pieces:
            for copy in g_copies[piece]:
                copy.wait_recv()
            start, size = PIECES[piece]
            for p in range(start, start + size):
                block = G[p, share(src), :]
                for d in range(1, nsrc):
                    block = block + R[d - 1, p]
                head = block.astype(jnp.bfloat16).astype(jnp.float32)
                heads.append(head)
                tails.append(block - head)
                chosen.append(ids[p:p + 1, :])
        row = lax.broadcasted_iota(jnp.int32, (pixels, len(chosen) * ys), 0)
        select = (row == jnp.concatenate(chosen, axis=1)).astype(jnp.float32).astype(jnp.bfloat16)
        for part in (heads, tails):
            part = jnp.concatenate(part, axis=0).astype(jnp.bfloat16)
            term = jnp.dot(select, part, preferred_element_type=jnp.float32)
            total = term if total is None else total + term
    for owner in range(n):
        T[owner % 2, owner // 2] = total[owner * PIX_DEV:(owner + 1) * PIX_DEV]
    swap = remote(T.at[1 - core], S, ss_sem.at[0], ss_sem.at[1], {"space": sibling})
    swap.start()
    swap.wait_recv()
    U[...] = T[core] + S[...]

    t_copies = [
        remote(U.at[lax.rem(chip + d, chips)], RT.at[d - 1], ts_sem.at[d - 1], tr_sem.at[d - 1],
               {"space": 2 * lax.rem(chip + d, chips) + core})
        for d in range(1, chips)
    ]
    for copy in t_copies:
        copy.start()
    result = U[chip]
    for d in range(1, chips):
        t_copies[d - 1].wait_recv()
        result = result + RT[d - 1]
    out[...] = result

    swap.wait_send()
    for copy in t_copies:
        copy.wait_send()
    for piece in g_copies:
        for copy in piece:
            copy.wait_send()
    pl.when(has_low)(lambda: [copy.wait_send() for copy in e_copies] and None)
    pl.when(has_high)(lambda: [copy.wait_send() for copy in h_copies] and None)


def solution(mesh):
    n, nsrc = mesh.shape["space"], mesh.shape["src"]

    def per_device(fwd, adj, eps, wave, foot):
        cx, ny, nz = eps.shape
        ys = foot.shape[1]
        f32 = jnp.float32
        raw, plane = (ny, nz), (ny // 8, 8, nz)

        def vmem(*shape):
            return pltpu.VMEM(shape, f32)

        dma = pltpu.SemaphoreType.DMA
        hbm = pl.BlockSpec(memory_space=pltpu.HBM)
        return pl.pallas_call(
            functools.partial(kernel, n, nsrc),
            out_shape=jax.ShapeDtypeStruct((PIX_DEV, nz), f32),
            in_specs=[hbm, hbm, hbm, pl.BlockSpec(memory_space=pltpu.SMEM), hbm],
            out_specs=pl.BlockSpec(memory_space=pltpu.VMEM),
            scratch_shapes=[
                pltpu.VMEM(foot.shape, jnp.int32), vmem(2, 3, cx, *raw), vmem(cx, *raw),
                vmem(2, 3, cx, *plane), vmem(cx + 4, *plane), vmem(ITERS, 2, 3, cx + 2, *plane),
                vmem(2, 3, cx + 1, *plane), vmem(2, 2, 3, 7, *plane), vmem(2, 2, 3, 7, *plane),
                vmem(3, 2, 2, 2, *plane), vmem(3, 2, 2, 2, *plane),
                vmem(*raw), vmem(*raw), vmem(2, 3, *raw), vmem(2, 2, *raw),
                vmem(*plane), vmem(*plane), vmem(2, *plane), vmem(2, 3, *plane), vmem(2, 8, 128),
                vmem(cx, *raw), vmem(nsrc - 1, cx, ys, nz),
                vmem(2, n // 2, PIX_DEV, nz), vmem(n // 2, PIX_DEV, nz), vmem(n // 2, PIX_DEV, nz),
                vmem(n // 2 - 1, PIX_DEV, nz),
                dma((4,)), dma((5,)), dma((5,)), dma((5,)), dma((5,)),
                dma((nsrc - 1, len(PIECES))), dma((nsrc - 1, len(PIECES))), dma((2,)), dma((n // 2 - 1,)), dma((n // 2 - 1,)),
            ],
            compiler_params=pltpu.CompilerParams(
                collective_id=0, has_side_effects=True, vmem_limit_bytes=60 * 1024 * 1024),
            cost_estimate=pl.CostEstimate(flops=30_000_000, bytes_accessed=2_000_000, transcendentals=0),
        )(fwd, adj, eps, wave, foot)

    in_specs = (
        P("src", None, "space", None, None),
        P("src", None, "space", None, None),
        P("space", None, None),
        P("src"),
        P("space", "src"),
    )
    return jax.shard_map(
        per_device, mesh=mesh, in_specs=in_specs, out_specs=P(("src", "space"), None), check_vma=False)
```

time: 26.5 us -> 28.1 us (1.060)
  Pallas kernels: 24.3 us -> 25.9 us
    pallas_call x1, Pallas kernels: 24.3 us -> 25.9 us  [per_device(): pl.pallas_call(functools.partial(kernel, n, nsrc), out_shape=jax.ShapeDty...]
where the time goes in v6:
time: 28.1 us; the launch traced here: 27.9 us
  Pallas kernels  25.9 us (92%)
  local copies, waits for them, and re-layouts  1.3 us (5%)
  between operations  0.66 us (2%)
    pallas_call x1, Pallas kernels, per_device(): pl.pallas_call(functools.partial(kernel, n, nsrc), out_shape=jax.ShapeDty...  25.9 us
    unnamed x1, local copies, waits for them, and re-layouts  1.3 us

profile of v6, /device:TPU:0, one launch (start us, length us, event | category | flops | bytes accessed | tf_op | source)
XLA Modules:
  0.0 27.9 jit_solution(13996115575150860125)
XLA Ops:
  0.7 25.9 %shard_map.55 = f32[16,128]{1,0:T(8,128)} custom-call(f32[1,3,8,64,128]{4,3,2,1,0:T(8,128)} %fwd.1, f32[1,3,8,64,128]{4,3,2,1,0:T(8,128)} %adj.1, f32[8,64,128]{2,1,0:T(8,128)} %eps.1, s32[1]{0:T(128)S(6)} %copy.7.wave, s32[8,32]{1,0:T(8,128)} %foot_hbm.1), custom_call_target="tpu_custom_call" | custom-call | flops 30000000 | bytes 2000000 | tf_op jit(solution)/shard_map/pallas_call | solution.py:382
  26.6 1.3 %copy.8 = f32[16,128]{1,0:T(8,128)} copy(f32[16,128]{1,0:T(8,128)} %shard_map.55) | data formatting | bytes 16384

commit v7 on v5

--- a/solution.py
+++ b/solution.py
@@ -169,17 +169,47 @@
     def planes(first, last, body):
         lax.fori_loop(first, last, lambda p, _: (body(p), 0)[1], 0)
 
+    folds = C.shape[1]
+    CHUNK = 2
+
+    def rows(ref, at, first, count):
+        if first < 0:
+            return jnp.concatenate([pltpu.roll(ref[(*at, pl.ds(folds - 1, 1))], 1, 1), ref[(*at, pl.ds(0, count - 1))]], axis=0)
+        if first + count > folds:
+            return jnp.concatenate([ref[(*at, pl.ds(first, count - 1))], pltpu.roll(ref[(*at, pl.ds(0, 1))], 7, 1)], axis=0)
+        return ref[(*at, pl.ds(first, count))]
+
+    def sweep_h(t, r, p):
+        for j in range(0, folds, CHUNK):
+            here = pl.ds(j, CHUNK)
+            e1, e2, e3 = (E[t, r, k, p, here] for k in range(3))
+            d1 = (rows(E, (t, r, 2, p), j + 1, CHUNK) - e3) - (ahead(e2, 1) - e2)
+            d2 = (ahead(e1, 1) - e1) - (E[t, r, 2, p + 1, here] - e3)
+            d3 = (E[t, r, 1, p + 1, here] - e2) - (rows(E, (t, r, 0, p), j + 1, CHUNK) - e1)
+            for k, d in enumerate((d1, d2, d3)):
+                H[r, k, p, here] = -d if t == 0 else H[r, k, p, here] - d
+
+    def sweep_e(t, r, p):
+        s = sig[r, t:t + 1, :]
+        for j in range(0, folds, CHUNK):
+            here = pl.ds(j, CHUNK)
+            c = C[p, here]
+            h1, h2, h3 = (H[r, k, p, here] for k in range(3))
+            d1 = (h3 - rows(H, (r, 2, p), j - 1, CHUNK)) - (h2 - behind(h2, 1))
+            d2 = (h1 - behind(h1, 1)) - (h3 - H[r, 2, p - 1, here])
+            d3 = (h2 - H[r, 1, p - 1, here]) - (h1 - rows(H, (r, 0, p), j - 1, CHUNK))
+            for k, d in enumerate((d1, d2, d3)):
+                E[t, r, k, p, here] = E[t - 1, r, k, p, here] + c * d - s * J[r, k, p, here]
+
     def sweep(t, first, last):
-        hs = [new_h(t, r, first) for r in range(2)]
         for r in range(2):
-            put(H, hs[r], r, first)
+            sweep_h(t, r, first)
 
         def body(p):
-            hs = [new_h(t, r, p) for r in range(2)]
-            es = [step_e(t + 1, r, p, e_at(t, r, p), hs[r], (H[r, 1, p - 1], H[r, 2, p - 1])) for r in range(2)]
             for r in range(2):
-                put(H, hs[r], r, p)
-                put_e(t + 1, r, p, es[r])
+                sweep_h(t, r, p)
+            for r in range(2):
+                sweep_e(t + 1, r, p)
 
         planes(first + 1, last, body)
 

time: 26.5 us -> 26.5 us (level)
  no operation moved by 1% of the time
where the time goes in v7:
time: 26.5 us; the launch traced here: 26.3 us
  Pallas kernels  24.3 us (92%)
  local copies, waits for them, and re-layouts  1.3 us (5%)
  between operations  0.66 us (2%)
    pallas_call x1, Pallas kernels, per_device(): pl.pallas_call(functools.partial(kernel, n, nsrc), out_shape=jax.ShapeDty...  24.3 us
    unnamed x1, local copies, waits for them, and re-layouts  1.3 us

profile of v7, /device:TPU:0, one launch (start us, length us, event | category | flops | bytes accessed | tf_op | source)
XLA Modules:
  0.0 26.3 jit_solution(10251111292245979609)
XLA Ops:
  0.7 24.3 %shard_map.55 = f32[16,128]{1,0:T(8,128)} custom-call(f32[1,3,8,64,128]{4,3,2,1,0:T(8,128)} %fwd.1, f32[1,3,8,64,128]{4,3,2,1,0:T(8,128)} %adj.1, f32[8,64,128]{2,1,0:T(8,128)} %eps.1, s32[1]{0:T(128)S(6)} %copy.7.wave, s32[8,32]{1,0:T(8,128)} %foot_hbm.1), custom_call_target="tpu_custom_call" | custom-call | flops 30000000 | bytes 2000000 | tf_op jit(solution)/shard_map/pallas_call | solution.py:439
  25.0 1.3 %copy.8 = f32[16,128]{1,0:T(8,128)} copy(f32[16,128]{1,0:T(8,128)} %shard_map.55) | data formatting | bytes 16384

commit v8 on v5

--- a/solution.py
+++ b/solution.py
@@ -9,7 +9,7 @@
 
 ITERS = 4
 PIX_DEV = 16
-PIECES = ((2, 4), (1, 1), (6, 1), (0, 1), (7, 1))
+PIECES = ((2, 4), (0, 2), (6, 2))
 MESH = pl.DeviceIdType.MESH
 
 
@@ -220,6 +220,18 @@
     start_h(3)
     sweep(1, 1, 6)
     sweep(2, 2, 5)
+
+    def product(p, more=None):
+        total = more
+        for t in range(ITERS):
+            for k in range(3):
+                term = E[t, 0, k, p] * E[ITERS - 1 - t, 1, k, p]
+                total = term if total is None else total + term
+        folds = total.shape[0]
+        for j in range(folds):
+            G[p, pl.ds(j, 8, stride=folds), :] = total[j]
+
+    lax.fori_loop(3, 5, lambda p, _: (product(p), 0)[1], 0)
 
     arrived(0, 1, 2)
     b_lo[...] = 0.25 * dealt(c_lo)
@@ -245,16 +257,6 @@
     q_hi[...] = b_hi[...] * for_high
     start_e(4)
     start_h(4)
-
-    def product(p, more=None):
-        total = more
-        for t in range(ITERS):
-            for k in range(3):
-                term = E[t, 0, k, p] * E[ITERS - 1 - t, 1, k, p]
-                total = term if total is None else total + term
-        folds = total.shape[0]
-        for j in range(folds):
-            G[p, pl.ds(j, 8, stride=folds), :] = total[j]
 
     def share(j):
         return pl.ds(pl.multiple_of(j * ys, 8), ys)
@@ -299,7 +301,7 @@
             put_e(t, r, p, e)
 
     runs(step2)
-    lax.fori_loop(2, 6, lambda p, _: (product(p), 0)[1], 0)
+    lax.fori_loop(0, 2, lambda i, _: (product(2 + 3 * i), 0)[1], 0)
     start_g(0)
     arrived(3)
 
@@ -330,19 +332,17 @@
 
     runs(step3)
     product(1)
-    start_g(1)
     product(6)
-    start_g(2)
     arrived(4)
     product(0, r_lo[...])
-    start_g(3)
+    start_g(1)
     product(7, r_hi[...])
-    start_g(4)
+    start_g(2)
 
     pixels = n * PIX_DEV
     ids = foot[...] - src * pixels
     total = None
-    for pieces in ((0,), (1, 2), (3, 4)):
+    for pieces in ((0,), (1, 2)):
         heads, tails, chosen = [], [], []
         for piece in pieces:
             for copy in g_copies[piece]:
@@ -374,10 +374,11 @@
                {"space": 2 * lax.rem(chip + d, chips) + core})
         for d in range(1, chips)
     ]
-    for copy in t_copies:
-        copy.start()
+    far_first = sorted(range(1, chips), key=lambda d: abs(2 * d - chips))
+    for d in far_first:
+        t_copies[d - 1].start()
     result = U[chip]
-    for d in range(1, chips):
+    for d in reversed(far_first):
         t_copies[d - 1].wait_recv()
         result = result + RT[d - 1]
     out[...] = result

time: 26.5 us -> 27.2 us (1.026)
  Pallas kernels: 24.3 us -> 25.1 us
    pallas_call x1, Pallas kernels: 24.3 us -> 25.1 us  [per_device(): pl.pallas_call(functools.partial(kernel, n, nsrc), out_shape=jax.ShapeDty...]
where the time goes in v8:
time: 27.2 us; the launch traced here: 27 us
  Pallas kernels  25.1 us (92%)
  local copies, waits for them, and re-layouts  1.3 us (5%)
  between operations  0.66 us (2%)
    pallas_call x1, Pallas kernels, per_device(): pl.pallas_call(functools.partial(kernel, n, nsrc), out_shape=jax.ShapeDty...  25.1 us
    unnamed x1, local copies, waits for them, and re-layouts  1.3 us

profile of v8, /device:TPU:0, one launch (start us, length us, event | category | flops | bytes accessed | tf_op | source)
XLA Modules:
  0.0 27.0 jit_solution(7200260756374647559)
XLA Ops:
  0.7 25.1 %shard_map.55 = f32[16,128]{1,0:T(8,128)} custom-call(f32[1,3,8,64,128]{4,3,2,1,0:T(8,128)} %fwd.1, f32[1,3,8,64,128]{4,3,2,1,0:T(8,128)} %adj.1, f32[8,64,128]{2,1,0:T(8,128)} %eps.1, s32[1]{0:T(128)S(6)} %copy.7.wave, s32[8,32]{1,0:T(8,128)} %foot_hbm.1), custom_call_target="tpu_custom_call" | custom-call | flops 30000000 | bytes 2000000 | tf_op jit(solution)/shard_map/pallas_call | solution.py:410
  25.7 1.3 %copy.8 = f32[16,128]{1,0:T(8,128)} copy(f32[16,128]{1,0:T(8,128)} %shard_map.55) | data formatting | bytes 16384
